TPU v7x, 32 devices: a whole 2x2x4 slice. The times are simulated.
32 devices in a mesh: gx: 4 (over y, x), gy: 8 (over z, core).
Axes of the slice: x: 2, y: 2, z: 4, core: 2. Of those that a mesh axis runs over, the one named last changes fastest.
Arguments:
- noise: float32 [8, 16, 4, 128], P('gx', 'gy'), may hold values from -4 to 4
- w_first: bfloat16 [16, 1, 3, 3, 3, 3], replicated, may hold values from -0.625 to 0.625
- b_first: float32 [16], replicated, may hold values from -2 to 2
- w_middle: bfloat16 [16, 16, 3, 3, 3, 3], replicated, may hold values from -0.15625 to 0.15625
- b_middle: float32 [16], replicated, may hold values from -2 to 2
- w_last: bfloat16 [2, 16, 3, 3, 3, 3], replicated, may hold values from -0.15625 to 0.15625
- b_last: float32 [2], replicated, may hold values from -2 to 2
Outputs:
- field: float32 [8, 16, 4, 128], P('gx', 'gy')
- noise_grad: float32 [8, 16, 4, 128], P('gx', 'gy')
- loss: float32 [], replicated
- w_first_grad: float32 [16, 1, 3, 3, 3, 3], replicated
- b_first_grad: float32 [16], replicated
- w_middle_grad: float32 [16, 16, 3, 3, 3, 3], replicated
- b_middle_grad: float32 [16], replicated
- w_last_grad: float32 [2, 16, 3, 3, 3, 3], replicated
- b_last_grad: float32 [2], replicated
All inputs are finite; a program needn't handle non-finite values.
Results may differ from a plain program's by a relative error of at most 0.0074.
Values may be sent and summed in bfloat16 or wider, within the bound.
A program may use at most 128 MiB of HBM per device.

v0:
```python
import jax
import jax.numpy as jnp
from jax import lax
from jax.sharding import PartitionSpec as P

HOPPING = 0.15
QUARTIC = 0.1


def padded_2(array, sides, width):
    for axis, dim in sides:
        devices, length = (lax.axis_size(axis), array.shape[dim])
        up = [(i, (i + 1) % devices) for i in range(devices)]
        down = [(j, i) for i, j in up]
        last = lax.slice_in_dim(array, length - width, length, axis=dim)
        leading = lax.slice_in_dim(array, 0, width, axis=dim)
        before = lax.ppermute(last, axis, up)
        after = lax.ppermute(leading, axis, down)
        array = jnp.concatenate([before, array, after], axis=dim)
    return array


def parity_mask(shape, offset_x, offset_y):
    index_x = jnp.arange(shape[0], dtype=jnp.int32) + offset_x
    index_y = jnp.arange(shape[1], dtype=jnp.int32) + offset_y
    index_t = jnp.arange(shape[2], dtype=jnp.int32)
    index_z = jnp.arange(shape[3], dtype=jnp.int32)
    summed = (
        index_x[:, None, None, None]
        + index_y[None, :, None, None]
        + index_t[None, None, :, None]
        + index_z[None, None, None, :]
    )
    return jnp.where(summed % 2 == 0, 1.0, 0.0).astype(jnp.float32)


def shifted_stack(padded):
    width_z = padded.shape[4] - 2
    return jnp.concatenate([padded[:, :, :, :, d : d + width_z] for d in range(3)], axis=0)


def conv_block(padded, kernel):
    width_x = padded.shape[1] - 2
    width_y = padded.shape[2] - 2
    width_t = padded.shape[3] - 2
    out_ch = kernel.shape[0]
    in_ch = kernel.shape[1]
    stacked = shifted_stack(padded)
    tap_weights = jnp.transpose(kernel, (2, 3, 4, 0, 5, 1)).reshape((3, 3, 3, out_ch, 3 * in_ch))
    summed = None
    for a in range(3):
        for b in range(3):
            for c in range(3):
                window = stacked[:, a : a + width_x, b : b + width_y, c : c + width_t]
                partial_out = jnp.einsum(
                    "ok,kxytz->oxytz",
                    tap_weights[a, b, c],
                    window,
                    preferred_element_type=jnp.float32,
                )
                summed = partial_out if summed is None else summed + partial_out
    return summed


def kernel_grad(padded, cotangent):
    width_x = cotangent.shape[1]
    width_y = cotangent.shape[2]
    width_t = cotangent.shape[3]
    out_ch = cotangent.shape[0]
    in_ch = padded.shape[0]
    stacked = shifted_stack(padded)
    pieces = []
    for a in range(3):
        for b in range(3):
            for c in range(3):
                window = stacked[:, a : a + width_x, b : b + width_y, c : c + width_t]
                pieces.append(
                    jnp.einsum(
                        "oxytz,kxytz->ok", cotangent, window, preferred_element_type=jnp.float32
                    )
                )
    gathered = jnp.stack(pieces).reshape((3, 3, 3, out_ch, 3, in_ch))
    return jnp.transpose(gathered, (3, 5, 0, 1, 2, 4))


def flip_kernel(kernel):
    return jnp.transpose(kernel[:, :, ::-1, ::-1, ::-1, ::-1], (1, 0, 2, 3, 4, 5))


def wrap_planes(field, depth):
    return jnp.pad(field, ((0, 0), (0, 0), (0, 0), (depth, depth), (depth, depth)), mode="wrap")


def channel_bias(bias):
    return bias[:, None, None, None, None]


def hidden_rims(field):
    return wrap_planes(padded_2(field, (("gx", 1), ("gy", 2)), 1), 1)


def channel_sum(cotangent):
    return jnp.sum(cotangent.astype(jnp.float32), axis=(1, 2, 3, 4))


def local(noise, w_first, b_first, w_middle, b_middle, w_last, b_last):
    sites = float(noise.size * lax.axis_size("gx") * lax.axis_size("gy"))
    frozen = parity_mask(
        noise.shape, lax.axis_index("gx") * noise.shape[0], lax.axis_index("gy") * noise.shape[1]
    )
    active = 1.0 - frozen
    inputs = (frozen * noise).astype(jnp.bfloat16)[None]
    padded_in = wrap_planes(padded_2(inputs, (("gx", 1), ("gy", 2)), 1), 1)
    hidden_one = jnp.tanh(conv_block(padded_in, w_first) + channel_bias(b_first)).astype(
        jnp.bfloat16
    )
    padded_one = hidden_rims(hidden_one)
    hidden_two = jnp.tanh(conv_block(padded_one, w_middle) + channel_bias(b_middle)).astype(
        jnp.bfloat16
    )
    padded_two = hidden_rims(hidden_two)
    head_out = conv_block(padded_two, w_last) + channel_bias(b_last)
    log_scale = jnp.tanh(head_out[0])
    offset_field = head_out[1]
    growth = jnp.exp(log_scale)
    field = frozen * noise + active * (noise * growth + offset_field)
    extended = padded_2(field, (("gx", 0), ("gy", 1)), 1)
    upward = (
        extended[2:, 1:-1] + extended[1:-1, 2:] + jnp.roll(field, -1, 2) + jnp.roll(field, -1, 3)
    )
    downward = (
        extended[:-2, 1:-1] + extended[1:-1, :-2] + jnp.roll(field, 1, 2) + jnp.roll(field, 1, 3)
    )
    squared = field * field
    density = (
        -2.0 * HOPPING * field * upward + squared + QUARTIC * (squared - 1.0) * (squared - 1.0)
    )
    local_loss = jnp.sum(-0.5 * noise * noise - active * log_scale + density)
    force_field = (
        -2.0 * HOPPING * (upward + downward) + 2.0 * field + 4.0 * QUARTIC * field * (squared - 1.0)
    )
    d_scale = active * (force_field * noise * growth - 1.0) * (1.0 - log_scale * log_scale)
    d_offset = active * force_field
    cot_last = jnp.stack([d_scale, d_offset], axis=0).astype(jnp.bfloat16)
    grad_last = kernel_grad(padded_two, cot_last)
    bias_last = channel_sum(cot_last)
    two_float = hidden_two.astype(jnp.float32)
    cot_middle = (
        conv_block(hidden_rims(cot_last), flip_kernel(w_last)) * (1.0 - two_float * two_float)
    ).astype(jnp.bfloat16)
    grad_middle = kernel_grad(padded_one, cot_middle)
    bias_middle = channel_sum(cot_middle)
    one_float = hidden_one.astype(jnp.float32)
    cot_first = (
        conv_block(hidden_rims(cot_middle), flip_kernel(w_middle)) * (1.0 - one_float * one_float)
    ).astype(jnp.bfloat16)
    grad_first = kernel_grad(padded_in, cot_first)
    bias_first = channel_sum(cot_first)
    grad_first, bias_first, grad_middle, bias_middle, grad_last, bias_last, local_loss = lax.psum(
        (grad_first, bias_first, grad_middle, bias_middle, grad_last, bias_last, local_loss),
        ("gx", "gy"),
    )
    d_inputs = conv_block(hidden_rims(cot_first), flip_kernel(w_first))
    noise_grad = frozen * d_inputs[0] + force_field * (frozen + active * growth) - noise
    return (
        field,
        noise_grad,
        local_loss / sites,
        grad_first / sites,
        bias_first / sites,
        grad_middle / sites,
        bias_middle / sites,
        grad_last / sites,
        bias_last / sites,
    )


def solution(mesh):
    placed = (P("gx", "gy", None, None), P(), P(), P(), P(), P(), P())
    return jax.shard_map(
        local,
        mesh=mesh,
        in_specs=placed,
        out_specs=(
            P("gx", "gy", None, None),
            P("gx", "gy", None, None),
            P(),
            P(),
            P(),
            P(),
            P(),
            P(),
            P(),
        ),
        check_vma=False,
    )
```

profile of v0, /device:TPU:0, one launch (start us, length us, event | category | flops | bytes accessed | tf_op | source)
XLA Modules:
  0.0 315.3 jit_solution(6824742966394179304)
XLA Ops:
  8.2 3.0 collective-permute-start
  12.2 1.5 collective-permute-done
  14.9 3.5 %collective-permute-start.3 = (bf16[1,4,1,4,128]{4,0,3,2,1:T(2,128)(2,1)S(1)}, bf16[1,4,1,4,128]{4,0,3,2,1:T(2,128)(2,1)S(1)}, u32[]{:S(2)}, u32[]{:S(2)}) collective-permute-start(bf16[1,4,1,4,128]{4,0,3,2,1:T(2,128)(2,1)S(1)} %get-tuple-element.222), channel_id=1, source_target_pairs={{1,0},{2,1},{3,2},{4,3},{5,4},{6,5},{7,6},{0,7},{9,8},{10,9},{11,1... | collective-permute-start | bytes 12296 | tf_op jit(solution)/shard_map/ppermute | solution.py:18
  28.5 2.4 collective-permute-start.4
  33.4 1.5 collective-permute-done.5
  35.0 3.5 %collective-permute-start.7 = (bf16[16,4,1,4,128]{4,0,3,2,1:T(8,128)(2,1)S(1)}, bf16[16,4,1,4,128]{4,0,3,2,1:T(8,128)(2,1)S(1)}, u32[]{:S(2)}, u32[]{:S(2)}) collective-permute-start(bf16[16,4,1,4,128]{4,0,3,2,1:T(8,128)(2,1)S(1)} %get-tuple-element.169), channel_id=1, source_target_pairs={{1,0},{2,1},{3,2},{4,3},{5,4},{6,5},{7,6},{0,7},{9,8},{10,9},{11,1... | collective-permute-start | bytes 196616 | tf_op jit(solution)/shard_map/ppermute | solution.py:18
  39.2 1.7 collective-permute-done.6
  46.0 1.5 collective-permute-start.8
  47.5 1.4 collective-permute-start.9
  49.0 1.6 fusion.607
  51.6 3.5 %collective-permute-start.11 = (bf16[16,4,1,4,128]{4,0,3,2,1:T(8,128)(2,1)S(1)}, bf16[16,4,1,4,128]{4,0,3,2,1:T(8,128)(2,1)S(1)}, u32[]{:S(2)}, u32[]{:S(2)}) collective-permute-start(bf16[16,4,1,4,128]{4,0,3,2,1:T(8,128)(2,1)S(1)} %get-tuple-element.167), channel_id=1, source_target_pairs={{1,0},{2,1},{3,2},{4,3},{5,4},{6,5},{7,6},{0,7},{9,8},{10,9},{11,1... | collective-permute-start | bytes 196616 | tf_op jit(solution)/shard_map/ppermute | solution.py:18
  55.3 1.7 collective-permute-done.10
  63.0 2.4 collective-permute-start.12
  66.8 3.2 %collective-permute-done.13 = f32[1,2,4,128]{3,2,1,0:T(4,128)S(1)} collective-permute-done((f32[1,2,4,128]{3,2,1,0:T(4,128)S(1)}, f32[1,2,4,128]{3,2,1,0:T(4,128)S(1)}, u32[]{:S(2)}, u32[]{:S(2)}) %collective-permute-start.13) | collective-permute-done | bytes 4128 | tf_op jit(solution)/shard_map/ppermute | solution.py:17
  70.0 2.2 collective-permute-start.14
  74.2 2.8 collective-permute-done.15
  77.3 2.9 collective-permute-start.17
  85.4 3.5 %collective-permute-start.19 = (bf16[2,4,1,4,128]{4,3,2,1,0:T(4,128)(2,1)S(1)}, bf16[2,4,1,4,128]{4,3,2,1,0:T(4,128)(2,1)S(1)}, u32[]{:S(2)}, u32[]{:S(2)}) collective-permute-start(bf16[2,4,1,4,128]{4,3,2,1,0:T(4,128)(2,1)S(1)} %get-tuple-element.216), channel_id=1, source_target_pairs={{1,0},{2,1},{3,2},{4,3},{5,4},{6,5},{7,6},{0,7},{9,8},{10,9},{11,1... | collective-permute-start | bytes 24584 | tf_op jit(solution)/shard_map/ppermute | solution.py:18
  97.1 2.9 collective-permute-start.21
  106.1 3.5 %collective-permute-start.23 = (bf16[16,4,1,4,128]{4,0,3,2,1:T(8,128)(2,1)S(1)}, bf16[16,4,1,4,128]{4,0,3,2,1:T(8,128)(2,1)S(1)}, u32[]{:S(2)}, u32[]{:S(2)}) collective-permute-start(bf16[16,4,1,4,128]{4,0,3,2,1:T(8,128)(2,1)S(1)} %get-tuple-element.165), channel_id=1, source_target_pairs={{1,0},{2,1},{3,2},{4,3},{5,4},{6,5},{7,6},{0,7},{9,8},{10,9},{11,1... | collective-permute-start | bytes 196616 | tf_op jit(solution)/shard_map/ppermute | solution.py:18
  109.6 124.0 %all-reduce.3.cloned.1.call-done = f32[16,16,3,3,3,3]{1,5,0,4,3,2:T(4,128)} async-done(((f32[16,16,3,3,3,3]{1,5,0,4,3,2:T(4,128)}), f32[16,16,3,3,3,3]{1,5,0,4,3,2:T(4,128)}) %all-reduce.3.cloned.1.call-update) | async-done | bytes 82960 | tf_op jit(solution)/shard_map/psum | solution.py:159
  246.5 43.9 %all-reduce = (f32[]{:T(128)}, f32[16,1,3,3,3,3]{0,4,3,2,5,1:T(4,128)S(1)}, f32[16]{0:T(128)S(1)}, f32[16]{0:T(128)S(1)}, f32[2,16,3,3,3,3]{1,5,0,4,3,2:T(4,128)S(1)}, /*index=5*/f32[2]{0:T(128)S(1)}) all-reduce(f32[]{:T(128)} %get-tuple-element.53, ...), channel_id=1, replica_groups=mesh['gx'=4,'gy'=8] {'gx','gy'}, use_global_device_ids=true, to_apply=%region_1.2 | all-reduce | flops 3923 | bytes 31384 | tf_op jit(solution)/shard_map/psum | solution.py:159
  291.5 2.4 collective-permute-start.25
  295.9 3.5 %collective-permute-start.27 = (bf16[16,4,1,4,128]{4,0,3,2,1:T(8,128)(2,1)S(1)}, bf16[16,4,1,4,128]{4,0,3,2,1:T(8,128)(2,1)S(1)}, u32[]{:S(2)}, u32[]{:S(2)}) collective-permute-start(bf16[16,4,1,4,128]{4,0,3,2,1:T(8,128)(2,1)S(1)} %get-tuple-element.163), channel_id=1, source_target_pairs={{1,0},{2,1},{3,2},{4,3},{5,4},{6,5},{7,6},{0,7},{9,8},{10,9},{11,1... | collective-permute-start | bytes 196616 | tf_op jit(solution)/shard_map/ppermute | solution.py:18
  (459 shorter events, 74.1 us)
Async XLA Ops:
  7.2 226.4 %all-reduce.3.cloned.1.call-start = ((), (), s32[]{:S(2)}) async-start(), calls=%async_computation | async-start | bytes 1769472 | tf_op jit(solution)/shard_map/psum | solution.py:159
  8.2 5.5 %collective-permute-start = (bf16[1,1,2,4,128]{4,0,3,2,1:T(2,128)(2,1)S(1)}, bf16[1,1,2,4,128]{4,0,3,2,1:T(2,128)(2,1)S(1)}, u32[]{:S(2)}, u32[]{:S(2)}) collective-permute-start(bf16[1,1,2,4,128]{4,0,3,2,1:T(2,128)(2,1)S(1)} %copy.1904), channel_id=1, source_target_pairs={{0,8},{8,16},{16,24},{24,0},{1,9},{9,17},{17,25},{25,1},{2,10},{10... | collective-permute-start | bytes 6152 | tf_op jit(solution)/shard_map/ppermute | solution.py:17
  14.9 7.2 %collective-permute-start.2 = (bf16[1,4,1,4,128]{4,0,3,2,1:T(2,128)(2,1)S(1)}, bf16[1,4,1,4,128]{4,0,3,2,1:T(2,128)(2,1)S(1)}, u32[]{:S(2)}, u32[]{:S(2)}) collective-permute-start(bf16[1,4,1,4,128]{4,0,3,2,1:T(2,128)(2,1)S(1)} %get-tuple-element.221), channel_id=1, source_target_pairs={{0,1},{1,2},{2,3},{3,4},{4,5},{5,6},{6,7},{7,0},{8,9},{9,10},{10,1... | collective-permute-start | bytes 12296 | tf_op jit(solution)/shard_map/ppermute | solution.py:17
  14.9 7.2 %collective-permute-start.3 = (bf16[1,4,1,4,128]{4,0,3,2,1:T(2,128)(2,1)S(1)}, bf16[1,4,1,4,128]{4,0,3,2,1:T(2,128)(2,1)S(1)}, u32[]{:S(2)}, u32[]{:S(2)}) collective-permute-start(bf16[1,4,1,4,128]{4,0,3,2,1:T(2,128)(2,1)S(1)} %get-tuple-element.222), channel_id=1, source_target_pairs={{1,0},{2,1},{3,2},{4,3},{5,4},{6,5},{7,6},{0,7},{9,8},{10,9},{11,1... | collective-permute-start | bytes 12296 | tf_op jit(solution)/shard_map/ppermute | solution.py:18
  28.5 4.9 %collective-permute-start.4 = (bf16[16,1,2,4,128]{4,0,3,2,1:T(8,128)(2,1)S(1)}, bf16[16,1,2,4,128]{4,0,3,2,1:T(8,128)(2,1)S(1)}, u32[]{:S(2)}, u32[]{:S(2)}) collective-permute-start(bf16[16,1,2,4,128]{4,0,3,2,1:T(8,128)(2,1)S(1)} %get-tuple-element.206), channel_id=1, source_target_pairs={{0,8},{8,16},{16,24},{24,0},{1,9},{9,17},{17,25},{25,1},{2,10},{10... | collective-permute-start | bytes 98312 | tf_op jit(solution)/shard_map/ppermute | solution.py:17
  34.9 5.9 %collective-permute-start.6 = (bf16[16,4,1,4,128]{4,0,3,2,1:T(8,128)(2,1)S(1)}, bf16[16,4,1,4,128]{4,0,3,2,1:T(8,128)(2,1)S(1)}, u32[]{:S(2)}, u32[]{:S(2)}) collective-permute-start(bf16[16,4,1,4,128]{4,0,3,2,1:T(8,128)(2,1)S(1)} %get-tuple-element.168), channel_id=1, source_target_pairs={{0,1},{1,2},{2,3},{3,4},{4,5},{5,6},{6,7},{7,0},{8,9},{9,10},{10,1... | collective-permute-start | bytes 196616 | tf_op jit(solution)/shard_map/ppermute | solution.py:17
  35.0 5.9 %collective-permute-start.7 = (bf16[16,4,1,4,128]{4,0,3,2,1:T(8,128)(2,1)S(1)}, bf16[16,4,1,4,128]{4,0,3,2,1:T(8,128)(2,1)S(1)}, u32[]{:S(2)}, u32[]{:S(2)}) collective-permute-start(bf16[16,4,1,4,128]{4,0,3,2,1:T(8,128)(2,1)S(1)} %get-tuple-element.169), channel_id=1, source_target_pairs={{1,0},{2,1},{3,2},{4,3},{5,4},{6,5},{7,6},{0,7},{9,8},{10,9},{11,1... | collective-permute-start | bytes 196616 | tf_op jit(solution)/shard_map/ppermute | solution.py:18
  46.0 4.9 %collective-permute-start.8 = (bf16[16,1,2,4,128]{4,0,3,2,1:T(8,128)(2,1)S(1)}, bf16[16,1,2,4,128]{4,0,3,2,1:T(8,128)(2,1)S(1)}, u32[]{:S(2)}, u32[]{:S(2)}) collective-permute-start(bf16[16,1,2,4,128]{4,0,3,2,1:T(8,128)(2,1)S(1)} %get-tuple-element.204), channel_id=1, source_target_pairs={{0,8},{8,16},{16,24},{24,0},{1,9},{9,17},{17,25},{25,1},{2,10},{10... | collective-permute-start | bytes 98312 | tf_op jit(solution)/shard_map/ppermute | solution.py:17
  51.5 5.5 %collective-permute-start.10 = (bf16[16,4,1,4,128]{4,0,3,2,1:T(8,128)(2,1)S(1)}, bf16[16,4,1,4,128]{4,0,3,2,1:T(8,128)(2,1)S(1)}, u32[]{:S(2)}, u32[]{:S(2)}) collective-permute-start(bf16[16,4,1,4,128]{4,0,3,2,1:T(8,128)(2,1)S(1)} %get-tuple-element.166), channel_id=1, source_target_pairs={{0,1},{1,2},{2,3},{3,4},{4,5},{5,6},{6,7},{7,0},{8,9},{9,10},{10,1... | collective-permute-start | bytes 196616 | tf_op jit(solution)/shard_map/ppermute | solution.py:17
  51.6 5.5 %collective-permute-start.11 = (bf16[16,4,1,4,128]{4,0,3,2,1:T(8,128)(2,1)S(1)}, bf16[16,4,1,4,128]{4,0,3,2,1:T(8,128)(2,1)S(1)}, u32[]{:S(2)}, u32[]{:S(2)}) collective-permute-start(bf16[16,4,1,4,128]{4,0,3,2,1:T(8,128)(2,1)S(1)} %get-tuple-element.167), channel_id=1, source_target_pairs={{1,0},{2,1},{3,2},{4,3},{5,4},{6,5},{7,6},{0,7},{9,8},{10,9},{11,1... | collective-permute-start | bytes 196616 | tf_op jit(solution)/shard_map/ppermute | solution.py:18
  65.4 4.5 %collective-permute-start.13 = (f32[1,2,4,128]{3,2,1,0:T(4,128)S(1)}, f32[1,2,4,128]{3,2,1,0:T(4,128)S(1)}, u32[]{:S(2)}, u32[]{:S(2)}) collective-permute-start(f32[1,2,4,128]{3,2,1,0:T(4,128)S(1)} %get-tuple-element.235), channel_id=1, source_target_pairs={{0,8},{8,16},{16,24},{24,0},{1,9},{9,17},{17,25},{25,1},{2,10},{10... | collective-permute-start | bytes 12296 | tf_op jit(solution)/shard_map/ppermute | solution.py:17
  72.1 4.9 %collective-permute-start.15 = (f32[4,1,4,128]{3,2,1,0:T(4,128)S(1)}, f32[4,1,4,128]{3,2,1,0:T(4,128)S(1)}, u32[]{:S(2)}, u32[]{:S(2)}) collective-permute-start(f32[4,1,4,128]{3,2,1,0:T(4,128)S(1)} %get-tuple-element.217), channel_id=1, source_target_pairs={{0,1},{1,2},{2,3},{3,4},{4,5},{5,6},{6,7},{7,0},{8,9},{9,10},{10,1... | collective-permute-start | bytes 24584 | tf_op jit(solution)/shard_map/ppermute | solution.py:17
  77.3 7.8 %collective-permute-start.16 = (bf16[2,1,2,4,128]{4,3,2,1,0:T(4,128)(2,1)S(1)}, bf16[2,1,2,4,128]{4,3,2,1,0:T(4,128)(2,1)S(1)}, u32[]{:S(2)}, u32[]{:S(2)}) collective-permute-start(bf16[2,1,2,4,128]{4,3,2,1,0:T(4,128)(2,1)S(1)} %get-tuple-element.225), channel_id=1, source_target_pairs={{0,8},{8,16},{16,24},{24,0},{1,9},{9,17},{17,25},{25,1},{2,10},{10... | collective-permute-start | bytes 12296 | tf_op jit(solution)/shard_map/ppermute | solution.py:17
  77.3 7.8 %collective-permute-start.17 = (bf16[2,1,2,4,128]{4,3,2,1,0:T(4,128)(2,1)S(1)}, bf16[2,1,2,4,128]{4,3,2,1,0:T(4,128)(2,1)S(1)}, u32[]{:S(2)}, u32[]{:S(2)}) collective-permute-start(bf16[2,1,2,4,128]{4,3,2,1,0:T(4,128)(2,1)S(1)} %get-tuple-element.226), channel_id=1, source_target_pairs={{8,0},{16,8},{24,16},{0,24},{9,1},{17,9},{25,17},{1,25},{10,2},{18... | collective-permute-start | bytes 12296 | tf_op jit(solution)/shard_map/ppermute | solution.py:18
  85.1 5.1 %collective-permute-start.18 = (bf16[2,4,1,4,128]{4,3,2,1,0:T(4,128)(2,1)S(1)}, bf16[2,4,1,4,128]{4,3,2,1,0:T(4,128)(2,1)S(1)}, u32[]{:S(2)}, u32[]{:S(2)}) collective-permute-start(bf16[2,4,1,4,128]{4,3,2,1,0:T(4,128)(2,1)S(1)} %get-tuple-element.215), channel_id=1, source_target_pairs={{0,1},{1,2},{2,3},{3,4},{4,5},{5,6},{6,7},{7,0},{8,9},{9,10},{10,1... | collective-permute-start | bytes 24584 | tf_op jit(solution)/shard_map/ppermute | solution.py:17
  85.4 4.9 %collective-permute-start.19 = (bf16[2,4,1,4,128]{4,3,2,1,0:T(4,128)(2,1)S(1)}, bf16[2,4,1,4,128]{4,3,2,1,0:T(4,128)(2,1)S(1)}, u32[]{:S(2)}, u32[]{:S(2)}) collective-permute-start(bf16[2,4,1,4,128]{4,3,2,1,0:T(4,128)(2,1)S(1)} %get-tuple-element.216), channel_id=1, source_target_pairs={{1,0},{2,1},{3,2},{4,3},{5,4},{6,5},{7,6},{0,7},{9,8},{10,9},{11,1... | collective-permute-start | bytes 24584 | tf_op jit(solution)/shard_map/ppermute | solution.py:18
  97.1 8.8 %collective-permute-start.20 = (bf16[16,1,2,4,128]{4,0,3,2,1:T(8,128)(2,1)S(1)}, bf16[16,1,2,4,128]{4,0,3,2,1:T(8,128)(2,1)S(1)}, u32[]{:S(2)}, u32[]{:S(2)}) collective-permute-start(bf16[16,1,2,4,128]{4,0,3,2,1:T(8,128)(2,1)S(1)} %get-tuple-element.200), channel_id=1, source_target_pairs={{0,8},{8,16},{16,24},{24,0},{1,9},{9,17},{17,25},{25,1},{2,10},{10... | collective-permute-start | bytes 98312 | tf_op jit(solution)/shard_map/ppermute | solution.py:17
  97.1 8.8 %collective-permute-start.21 = (bf16[16,1,2,4,128]{4,0,3,2,1:T(8,128)(2,1)S(1)}, bf16[16,1,2,4,128]{4,0,3,2,1:T(8,128)(2,1)S(1)}, u32[]{:S(2)}, u32[]{:S(2)}) collective-permute-start(bf16[16,1,2,4,128]{4,0,3,2,1:T(8,128)(2,1)S(1)} %get-tuple-element.199), channel_id=1, source_target_pairs={{8,0},{16,8},{24,16},{0,24},{9,1},{17,9},{25,17},{1,25},{10,2},{18... | collective-permute-start | bytes 98312 | tf_op jit(solution)/shard_map/ppermute | solution.py:18
  106.0 129.9 %collective-permute-start.22 = (bf16[16,4,1,4,128]{4,0,3,2,1:T(8,128)(2,1)S(1)}, bf16[16,4,1,4,128]{4,0,3,2,1:T(8,128)(2,1)S(1)}, u32[]{:S(2)}, u32[]{:S(2)}) collective-permute-start(bf16[16,4,1,4,128]{4,0,3,2,1:T(8,128)(2,1)S(1)} %get-tuple-element.164), channel_id=1, source_target_pairs={{0,1},{1,2},{2,3},{3,4},{4,5},{5,6},{6,7},{7,0},{8,9},{9,10},{10,1... | collective-permute-start | bytes 196616 | tf_op jit(solution)/shard_map/ppermute | solution.py:17
  106.1 129.8 %collective-permute-start.23 = (bf16[16,4,1,4,128]{4,0,3,2,1:T(8,128)(2,1)S(1)}, bf16[16,4,1,4,128]{4,0,3,2,1:T(8,128)(2,1)S(1)}, u32[]{:S(2)}, u32[]{:S(2)}) collective-permute-start(bf16[16,4,1,4,128]{4,0,3,2,1:T(8,128)(2,1)S(1)} %get-tuple-element.165), channel_id=1, source_target_pairs={{1,0},{2,1},{3,2},{4,3},{5,4},{6,5},{7,6},{0,7},{9,8},{10,9},{11,1... | collective-permute-start | bytes 196616 | tf_op jit(solution)/shard_map/ppermute | solution.py:18
  291.0 4.8 %collective-permute-start.24 = (bf16[16,1,2,4,128]{4,0,3,2,1:T(8,128)(2,1)S(1)}, bf16[16,1,2,4,128]{4,0,3,2,1:T(8,128)(2,1)S(1)}, u32[]{:S(2)}, u32[]{:S(2)}) collective-permute-start(bf16[16,1,2,4,128]{4,0,3,2,1:T(8,128)(2,1)S(1)} %get-tuple-element.198), channel_id=1, source_target_pairs={{0,8},{8,16},{16,24},{24,0},{1,9},{9,17},{17,25},{25,1},{2,10},{10... | collective-permute-start | bytes 98312 | tf_op jit(solution)/shard_map/ppermute | solution.py:17
  291.5 4.3 %collective-permute-start.25 = (bf16[16,1,2,4,128]{4,0,3,2,1:T(8,128)(2,1)S(1)}, bf16[16,1,2,4,128]{4,0,3,2,1:T(8,128)(2,1)S(1)}, u32[]{:S(2)}, u32[]{:S(2)}) collective-permute-start(bf16[16,1,2,4,128]{4,0,3,2,1:T(8,128)(2,1)S(1)} %get-tuple-element.197), channel_id=1, source_target_pairs={{8,0},{16,8},{24,16},{0,24},{9,1},{17,9},{25,17},{1,25},{10,2},{18... | collective-permute-start | bytes 98312 | tf_op jit(solution)/shard_map/ppermute | solution.py:18
  295.8 6.1 %collective-permute-start.26 = (bf16[16,4,1,4,128]{4,0,3,2,1:T(8,128)(2,1)S(1)}, bf16[16,4,1,4,128]{4,0,3,2,1:T(8,128)(2,1)S(1)}, u32[]{:S(2)}, u32[]{:S(2)}) collective-permute-start(bf16[16,4,1,4,128]{4,0,3,2,1:T(8,128)(2,1)S(1)} %get-tuple-element.162), channel_id=1, source_target_pairs={{0,1},{1,2},{2,3},{3,4},{4,5},{5,6},{6,7},{7,0},{8,9},{9,10},{10,1... | collective-permute-start | bytes 196616 | tf_op jit(solution)/shard_map/ppermute | solution.py:17
  295.9 6.0 %collective-permute-start.27 = (bf16[16,4,1,4,128]{4,0,3,2,1:T(8,128)(2,1)S(1)}, bf16[16,4,1,4,128]{4,0,3,2,1:T(8,128)(2,1)S(1)}, u32[]{:S(2)}, u32[]{:S(2)}) collective-permute-start(bf16[16,4,1,4,128]{4,0,3,2,1:T(8,128)(2,1)S(1)} %get-tuple-element.163), channel_id=1, source_target_pairs={{1,0},{2,1},{3,2},{4,3},{5,4},{6,5},{7,6},{0,7},{9,8},{10,9},{11,1... | collective-permute-start | bytes 196616 | tf_op jit(solution)/shard_map/ppermute | solution.py:18
  (45 other events, 112.1 us)
Sparse Core Ops, SparseCore 0:
  106.0 127.5 all-reduce.2
where the time goes:
time: 316 us; the launch traced here: 315 us
  waiting for transfers between devices  145 us (46%)
  starting transfers between devices  45.1 us (14%)
  blocking collectives  43.9 us (14%)
  matrix products  42 us (13%)
  between operations  16.9 us (5%)
  local copies, waits for them, and re-layouts  13.3 us (4%)
  other arithmetic  9.33 us (3%)
    psum x1, waiting for transfers between devices, local(): lax.psum((grad_first, bias_first, grad_middle, bias_middle, grad_last, bi...  124 us
    psum x1, blocking collectives, local(): lax.psum((grad_first, bias_first, grad_middle, bias_middle, grad_last, bi...  43.9 us
    ppermute x14, starting transfers between devices, padded_2(): after = lax.ppermute(leading, axis, down)  37 us
    dot_general x162, matrix products, conv_block(): jnp.einsum('ok,kxytz->oxytz', tap_weights[a, b, c], window, preferred_ele...  28.9 us
    ppermute x14, waiting for transfers between devices, padded_2(): before = lax.ppermute(last, axis, up)  15 us
    dot_general x81, matrix products, kernel_grad(): jnp.einsum('oxytz,kxytz->ok', cotangent, window, preferred_element_type=j...  13 us
    ppermute x14, starting transfers between devices, padded_2(): before = lax.ppermute(last, axis, up)  8.05 us
  transfers between devices with their start and end apart: 29, of which 15 were waited for; matrix products, arithmetic and copies ran while one was open for 7% of the time, Pallas kernels for 0%

commit v1 on v0

v1 whole, which is shorter than its diff:
```python
import functools

import jax
import jax.numpy as jnp
from jax import lax
from jax.experimental import pallas as pl
from jax.experimental.pallas import tpu as pltpu
from jax.sharding import PartitionSpec as P

HOPPING = 0.15
QUARTIC = 0.1
MESH = pl.DeviceIdType.MESH
F32 = jnp.float32
BF16 = jnp.bfloat16
OFFSETS = [(dx, dy) for dx in range(-2, 3) for dy in range(-2, 3) if (dx, dy) != (0, 0)]
PAIRS = [(y, t) for y in range(2) for t in range(4)]


def dot(a, b):
    return jnp.dot(a, b, preferred_element_type=F32)


def dot_nt(a, b):
    return lax.dot_general(a, b, (((1,), (1,)), ((), ())), preferred_element_type=F32)


def roll_z(v, step):
    if step == 0:
        return v
    parts = [
        pltpu.roll(v[:, k : k + 128], (-step) % 128, 1) for k in range(0, v.shape[1], 128)
    ]
    return parts[0] if len(parts) == 1 else jnp.concatenate(parts, axis=1)


def iota(shape, dim):
    return lax.broadcasted_iota(jnp.int32, shape, dim)


def select_matrix(rows, target):
    lanes = target.shape[1]
    return jnp.where(iota((rows, lanes), 0) == target, 1.0, 0.0).astype(BF16)


def taps_channels(y, t):
    lane = iota((1, 256), 1)
    b = (lane >> 6) - y
    c = (((lane >> 4) & 3) - t + 1) & 3
    ok = (b >= 0) & (b <= 2) & (c <= 2)
    return select_matrix(144, jnp.where(ok, b * 48 + c * 16 + (lane & 15), -1))


def taps_single(y, t):
    lane = iota((1, 144), 1)
    b = ((lane >> 2) & 3) - y
    c = ((lane & 3) - t + 1) & 3
    ok = (b >= 0) & (b <= 2) & (c <= 2)
    return select_matrix(81, jnp.where(ok, (lane >> 4) * 9 + b * 3 + c, -1))


def taps_heads(y, t):
    lane = iota((1, 432), 1)
    group = sum((lane >= 48 * k).astype(jnp.int32) for k in range(1, 9))
    rest = lane - 48 * group
    b = 2 * (rest >> 4) + ((rest >> 2) & 1) - y - 1
    c = ((rest & 3) - t + 1) & 3
    ok = (b >= 0) & (b <= 2) & (c <= 2)
    target = group * 18 + ((rest >> 3) & 1) * 9 + b * 3 + c
    return select_matrix(162, jnp.where(ok, target, -1))


def split(v):
    high = v.astype(BF16)
    return high, (v - high.astype(F32)).astype(BF16)


def kernel(
    nx, ny, noise_ref, wall_ref, w1_ref, w3t_ref, b1_ref, b2_ref, b3_ref,
    field_ref, ngrad_ref, pack_ref,
    win, inr, clw, clr, g2, g2t, g1, g3t, h1, h2, cm, cf, fld,
    send_a, recv_a, send_b, recv_b,
):
    ix, iy = lax.axis_index("gx"), lax.axis_index("gy")

    def peer(dx, dy):
        return (lax.rem(ix + dx + 2 * nx, nx), lax.rem(iy + dy + 2 * ny, ny))

    def exchange(ref, rows, send, recv):
        copies = []
        for k, (dx, dy) in enumerate(OFFSETS):
            copies.append(
                pltpu.make_async_remote_copy(
                    src_ref=ref.at[pl.ds(2 * rows, rows), pl.ds(512, 256)],
                    dst_ref=ref.at[pl.ds((2 - dy) * rows, rows), pl.ds((2 - dx) * 256, 256)],
                    send_sem=send.at[k],
                    recv_sem=recv.at[k],
                    device_id=peer(dx, dy),
                    device_id_type=MESH,
                )
            )
        return copies

    for x in range(2):
        for y in range(2):
            win[pl.ds(16 + 4 * y, 4), pl.ds(512 + 128 * x, 128)] = noise_ref[x, y]

    barrier = pltpu.get_barrier_semaphore()
    for dx, dy in OFFSETS:
        pl.semaphore_signal(barrier, inc=1, device_id=peer(dx, dy), device_id_type=MESH)
    pl.semaphore_wait(barrier, len(OFFSETS))
    first = exchange(win, 8, send_a, recv_a)
    for copy in first:
        copy.start()

    wall = wall_ref[...]
    w1 = w1_ref[...]
    w3t = w3t_ref[...]
    small = []
    for n, (y, t) in enumerate(PAIRS):
        full = dot(wall, taps_channels(y, t)).astype(BF16)
        for a in range(3):
            for d in range(3):
                g2[a, pl.ds(d * 128 + n * 16, 16), :] = full[(3 * a + d) * 16 : (3 * a + d) * 16 + 16]
                g2t[a, pl.ds(d * 128 + n * 16, 16), :] = full[
                    144 + (3 * a + d) * 16 : 144 + (3 * a + d) * 16 + 16
                ]
        small.append(full[288:320])
        g1[pl.ds(n * 16, 16), :] = dot(w1, taps_single(y, t)).astype(BF16)
        g3t[pl.ds(n * 16, 16), :] = dot(w3t, taps_heads(y, t)).astype(BF16)
    small = jnp.concatenate(small, axis=0)
    row = iota((216, 256), 0)
    order = jnp.where((row & 7) * 32 + (row >> 3) == iota((216, 256), 1), 1.0, 0.0).astype(BF16)
    small = dot(order, small).astype(BF16)
    g3 = [small[48 * a : 48 * a + 48] for a in range(3)]
    g1t = [small[144 + 24 * a : 168 + 24 * a] for a in range(3)]
    b1, b2 = b1_ref[...], b2_ref[...]
    bias1 = jnp.concatenate([b1] * 8, axis=0)
    bias2 = jnp.concatenate([b2] * 8, axis=0)

    for copy in first:
        copy.wait()

    noise_all = win[...]
    parity = (iota((40, 1280), 0) >> 2) + iota((40, 1280), 0) + (iota((40, 1280), 1) >> 7) + iota((40, 1280), 1)
    inputs = jnp.where((parity & 1) == 0, noise_all, 0.0).astype(BF16).astype(F32)
    for d in range(3):
        inr[d] = roll_z(inputs, d - 1)
    for j in range(4):
        stack = jnp.concatenate(
            [
                inr[d, pl.ds(8 * j, 16), pl.ds(128 * a, 1024)]
                for d in range(3)
                for a in range(3)
            ],
            axis=0,
        ).astype(BF16)
        h1[pl.ds(128 * j, 128), :] = jnp.tanh(dot(g1[...], stack) + bias1).astype(BF16)

    def conv(mats, ref, start, width, rows):
        out = None
        for a in range(3):
            part = dot(mats[a], ref[pl.ds(start, 256), pl.ds(128 * a, width)])
            out = part if out is None else out + part
        total = out[rows : 2 * rows]
        for d in (0, 2):
            total = total + roll_z(out[d * rows : (d + 1) * rows], d - 1)
        return total

    for k in range(3):
        h2[pl.ds(128 * k, 128), :] = jnp.tanh(
            conv(g2, h1, 128 * k, 768, 128) + bias2
        ).astype(BF16)

    scales, growths = [], []
    for k in range(2):
        head = conv(g3, h2, 128 * k, 512, 16)
        log_scale = jnp.tanh(head[:8] + b3_ref[0])
        offset = head[8:] + b3_ref[1]
        noise = win[pl.ds(12 + 8 * k, 8), pl.ds(384, 512)]
        growth = jnp.exp(log_scale)
        r, l = iota((8, 512), 0), iota((8, 512), 1)
        even = (((r >> 2) + r + (l >> 7) + l) & 1) == 0
        fld[pl.ds(8 * k, 8), :] = jnp.where(even, noise, noise * growth + offset)
        scales.append(log_scale)
    log_scale = jnp.concatenate([scales[0][4:], scales[1][:4]], axis=0)[:, 128:384]
    growth = jnp.exp(log_scale)
    noise = win[pl.ds(16, 8), pl.ds(512, 256)]
    field = fld[pl.ds(4, 8), pl.ds(128, 256)]
    r, l = iota((8, 256), 0), iota((8, 256), 1)
    frozen = (((r >> 2) + r + (l >> 7) + l) & 1) == 0
    active = jnp.where(frozen, 0.0, 1.0)
    t_up = jnp.concatenate([field[1:4], field[0:1], field[5:8], field[4:5]], axis=0)
    t_down = jnp.concatenate([field[3:4], field[0:3], field[7:8], field[4:7]], axis=0)
    upward = (
        fld[pl.ds(4, 8), pl.ds(256, 256)] + fld[pl.ds(8, 8), pl.ds(128, 256)]
        + t_up + roll_z(field, 1)
    )
    downward = (
        fld[pl.ds(4, 8), pl.ds(0, 256)] + fld[pl.ds(0, 8), pl.ds(128, 256)]
        + t_down + roll_z(field, -1)
    )
    squared = field * field
    density = (
        -2.0 * HOPPING * field * upward + squared + QUARTIC * (squared - 1.0) * (squared - 1.0)
    )
    loss = jnp.sum(
        jnp.sum(-0.5 * noise * noise - active * log_scale + density, axis=1, keepdims=True),
        axis=0, keepdims=True,
    )
    force = (
        -2.0 * HOPPING * (upward + downward) + 2.0 * field + 4.0 * QUARTIC * field * (squared - 1.0)
    )
    d_scale = active * (force * noise * growth - 1.0) * (1.0 - log_scale * log_scale)
    d_offset = active * force
    cot_last = jnp.concatenate([d_scale, d_offset], axis=0).astype(BF16)
    clw[pl.ds(32, 16), pl.ds(512, 256)] = cot_last
    second = exchange(clw, 16, send_b, recv_b)
    for copy in second:
        copy.start()
    for x in range(2):
        for y in range(2):
            field_ref[x, y] = field[4 * y : 4 * y + 4, 128 * x : 128 * x + 128]

    cot_f = cot_last.astype(F32)
    bias_last = jnp.sum(cot_f, axis=1, keepdims=True)
    bias_last = jnp.concatenate(
        [jnp.sum(bias_last[:8], axis=0, keepdims=True), jnp.sum(bias_last[8:], axis=0, keepdims=True)],
        axis=0,
    )
    turned = jnp.concatenate([roll_z(cot_f, 1 - d) for d in range(3)], axis=0).astype(BF16)
    row, col = iota((64, 48), 0), iota((64, 48), 1)
    order = jnp.where((row & 7) * 8 + (row >> 3) == col, 1.0, 0.0).astype(BF16)
    turned = dot(order, turned).astype(BF16)
    last_products = [
        dot_nt(turned, h2[pl.ds(64, 256), pl.ds(128 * (a + 1), 256)]) for a in range(3)
    ]

    for copy in second:
        copy.wait()

    everywhere = clw[...].astype(F32)
    for d in range(3):
        clr[d] = roll_z(everywhere, d - 1).astype(BF16)
    for k in range(3):
        stack = jnp.concatenate(
            [
                clr[d, pl.ds(16 * k, 48), pl.ds(128 * (a + 1), 768)]
                for d in range(3)
                for a in range(3)
            ],
            axis=0,
        )
        hidden = h2[pl.ds(128 * k, 128), :].astype(F32)
        cm[pl.ds(128 * k, 128), :] = (dot(g3t[...], stack) * (1.0 - hidden * hidden)).astype(BF16)

    mine = cm[pl.ds(128, 128), pl.ds(256, 256)].astype(F32)
    bias_mid = jnp.sum(mine, axis=1, keepdims=True)
    bias_mid = sum(bias_mid[16 * n : 16 * n + 16] for n in range(8))
    turned = jnp.concatenate([roll_z(mine, 1 - d) for d in range(3)], axis=0).astype(BF16)
    products = [dot_nt(turned, h1[pl.ds(128, 256), pl.ds(128 * (a + 2), 256)]) for a in range(3)]
    folded = None
    for n, (y, t) in enumerate(PAIRS):
        piece = jnp.concatenate(
            [
                products[a][d * 128 + n * 16 : d * 128 + n * 16 + 16]
                for a in range(3)
                for d in range(3)
            ]
            + [last_products[a][8 * n : 8 * n + 8] for a in range(3)],
            axis=0,
        )
        high, low = split(piece)
        matrix = taps_channels(y, t)
        part = dot_nt(high, matrix) + dot_nt(low, matrix)
        folded = part if folded is None else folded + part
    pack_ref[pl.ds(0, 168), :] = folded

    for k in range(2):
        hidden = h1[pl.ds(128 * (k + 1), 128), pl.ds(256, 512)].astype(F32)
        cf[pl.ds(128 * k, 128), :] = (
            conv(g2t, cm, 128 * k, 512, 128) * (1.0 - hidden * hidden)
        ).astype(BF16)
    mine = cf[pl.ds(64, 128), pl.ds(128, 256)]
    bias_first = jnp.sum(mine.astype(F32), axis=1, keepdims=True)
    bias_first = sum(bias_first[16 * n : 16 * n + 16] for n in range(8))
    stack = jnp.concatenate(
        [inr[d, pl.ds(12, 16), pl.ds(128 * (a + 3), 256)] for d in range(3) for a in range(3)], axis=0
    ).astype(BF16)
    product = dot_nt(mine, stack)
    folded = None
    for n, (y, t) in enumerate(PAIRS):
        high, low = split(product[16 * n : 16 * n + 16])
        matrix = taps_single(y, t)
        part = dot_nt(high, matrix) + dot_nt(low, matrix)
        folded = part if folded is None else folded + part
    pad = jnp.zeros((14, 1), F32)
    pack_ref[pl.ds(168, 16), :] = jnp.concatenate(
        [
            folded, bias_mid, bias_first, jnp.concatenate([bias_last, pad], axis=0),
            jnp.concatenate([loss, pad, jnp.zeros((1, 1), F32)], axis=0), jnp.zeros((16, 59), F32),
        ],
        axis=1,
    )

    back = conv(g1t, cf, 0, 256, 8)
    result = jnp.where(frozen, back, 0.0) + force * jnp.where(frozen, 1.0, growth) - noise
    for x in range(2):
        for y in range(2):
            ngrad_ref[x, y] = result[4 * y : 4 * y + 4, 128 * x : 128 * x + 128]


def local(nx, ny, noise, w_first, b_first, w_middle, b_middle, w_last, b_last):
    sites = float(noise.size * nx * ny)
    wm = jnp.transpose(w_middle, (2, 5, 0, 3, 4, 1)).reshape(144, 144)
    wmt = jnp.transpose(w_middle[:, :, ::-1, ::-1, ::-1, ::-1], (2, 5, 1, 3, 4, 0)).reshape(144, 144)
    wl = jnp.transpose(w_last, (2, 5, 0, 3, 4, 1)).reshape(18, 144)
    wft = jnp.transpose(w_first[:, 0, ::-1, ::-1, ::-1, ::-1], (1, 4, 2, 3, 0)).reshape(9, 144)
    wall = jnp.concatenate([wm, wmt, wl, wft, jnp.zeros((5, 144), BF16)], axis=0)
    w1 = jnp.transpose(w_first[:, 0], (0, 4, 1, 2, 3)).reshape(16, 81)
    w3t = jnp.transpose(w_last[:, :, ::-1, ::-1, ::-1, ::-1], (1, 5, 2, 0, 3, 4)).reshape(16, 162)
    vmem = pl.BlockSpec(memory_space=pltpu.VMEM)
    smem = pl.BlockSpec(memory_space=pltpu.SMEM)
    field, ngrad, pack = pl.pallas_call(
        functools.partial(kernel, nx, ny),
        out_shape=(
            jax.ShapeDtypeStruct(noise.shape, F32),
            jax.ShapeDtypeStruct(noise.shape, F32),
            jax.ShapeDtypeStruct((184, 144), F32),
        ),
        in_specs=[vmem] * 6 + [smem],
        out_specs=(vmem, vmem, vmem),
        scratch_shapes=[
            pltpu.VMEM((40, 1280), F32),
            pltpu.VMEM((3, 40, 1280), F32),
            pltpu.VMEM((80, 1280), BF16),
            pltpu.VMEM((3, 80, 1280), BF16),
            pltpu.VMEM((3, 384, 256), BF16),
            pltpu.VMEM((3, 384, 256), BF16),
            pltpu.VMEM((128, 144), BF16),
            pltpu.VMEM((128, 432), BF16),
            pltpu.VMEM((512, 1024), BF16),
            pltpu.VMEM((384, 768), BF16),
            pltpu.VMEM((384, 768), BF16),
            pltpu.VMEM((256, 512), BF16),
            pltpu.VMEM((16, 512), F32),
        ]
        + [pltpu.SemaphoreType.DMA((24,))] * 4,
        compiler_params=pltpu.CompilerParams(
            collective_id=0, has_side_effects=True, vmem_limit_bytes=32 * 1024 * 1024
        ),
    )(noise, wall, w1, w3t, b_first[:, None], b_middle[:, None], b_last)
    pack = lax.psum(pack, ("gx", "gy")) / sites
    middle = jnp.transpose(pack[:144].reshape(3, 3, 16, 3, 3, 16), (2, 5, 0, 3, 4, 1))
    last = jnp.transpose(
        pack[144:168].reshape(3, 8, 3, 3, 16)[:, :6].reshape(3, 3, 2, 3, 3, 16), (2, 5, 0, 3, 4, 1)
    )
    extra = pack[168:184]
    first = jnp.transpose(extra[:, :81].reshape(16, 3, 3, 3, 3), (0, 2, 3, 4, 1))[:, None]
    return (
        field, ngrad, extra[0, 84], first, extra[:, 82], middle, extra[:, 81], last, extra[:2, 83],
    )


def solution(mesh):
    placed = (P("gx", "gy", None, None), P(), P(), P(), P(), P(), P())
    return jax.shard_map(
        functools.partial(local, mesh.shape["gx"], mesh.shape["gy"]),
        mesh=mesh,
        in_specs=placed,
        out_specs=(
            P("gx", "gy", None, None), P("gx", "gy", None, None), P(), P(), P(), P(), P(), P(), P(),
        ),
        check_vma=False,
    )
```

time: 316 us -> 173 us (0.55)
  starting transfers between devices: 45.1 us -> 0.04 us
  blocking collectives: 43.9 us -> 0 us
  matrix products: 42 us -> 0 us
  Pallas kernels: 0 us -> 25.7 us
  waiting for transfers between devices: 145 us -> 120 us
  other arithmetic: 9.33 us -> 0.94 us
    ppermute x28 -> x0, starting transfers between devices: 45 us -> none  [the longest x14 37 us: padded_2(): after = lax.ppermute(leading, axis, down)]
    psum x1 -> x0, blocking collectives: 43.9 us -> none  [local(): lax.psum((grad_first, bias_first, grad_middle, bias_middle, grad_last, bi...]
    dot_general x243 -> x0, matrix products: 42 us -> none  [the longest x162 28.9 us: conv_block(): jnp.einsum('ok,kxytz->oxytz', tap_weights[a, b, c], window, preferred_ele...]
    pallas_call x0 -> x1, Pallas kernels: none -> 25.7 us  [local(): pl.pallas_call(functools.partial(kernel, nx, ny), out_shape=(jax.ShapeDty...]
    ppermute x28 -> x0, waiting for transfers between devices: 20.8 us -> none  [the longest x14 15 us: padded_2(): before = lax.ppermute(last, axis, up)]
    psum x1, waiting for transfers between devices: 124 us -> 120 us  [local(): pack = lax.psum(pack, ('gx', 'gy')) / sites]
    concatenate x25 -> x0, other arithmetic: 3.56 us -> none  [the longest x11 2.52 us: wrap_planes(): jnp.pad(field, ((0, 0), (0, 0), (0, 0), (depth, depth), (depth, depth)),...]
    slice x33 -> x9, local copies, waits for them, and re-layouts: 5.61 us -> 2.32 us  [the longest x1 0.7 us: local(): extra[:, 81]]
  transfers between devices with their start and end apart: 29 -> 1, of which waited for: 15 -> 1; matrix products, arithmetic and copies ran while one was open for 7% -> 0% of each run, Pallas kernels for 0% -> 0%
where the time goes in v1:
time: 173 us; the launch traced here: 172 us
  waiting for transfers between devices  120 us (69%)
  Pallas kernels  25.7 us (15%)
  between operations  14.2 us (8%)
  local copies, waits for them, and re-layouts  11.3 us (7%)
    psum x1, waiting for transfers between devices, local(): pack = lax.psum(pack, ('gx', 'gy')) / sites  120 us
    pallas_call x1, Pallas kernels, local(): pl.pallas_call(functools.partial(kernel, nx, ny), out_shape=(jax.ShapeDty...  25.7 us
    unnamed x20, local copies, waits for them, and re-layouts  5.07 us
  transfers between devices with their start and end apart: 1, of which 1 were waited for; matrix products, arithmetic and copies ran while one was open for 0% of the time, Pallas kernels for 0%

profile of v1, /device:TPU:0, one launch (start us, length us, event | category | flops | bytes accessed | tf_op | source)
XLA Modules:
  0.0 172.4 jit_solution(10241444136752742680)
XLA Ops:
  7.2 0.6 copy-done.6
  7.9 0.7 copy-done.7
  8.7 0.9 rev.10
  9.8 0.5 copy-done.4
  10.7 0.2 copy.28
  10.9 0.2 reshape.49
  11.2 0.2 copy.27
  11.4 0.2 reshape.48
  11.7 0.2 concatenate.3.wall_ref
  11.8 0.5 copy-done
  12.3 25.7 %shard_map.142 = (f32[2,2,4,128]{3,2,1,0:T(4,128)S(1)}, f32[2,2,4,128]{3,2,1,0:T(4,128)S(1)}, f32[184,144]{1,0:T(8,128)}) custom-call(f32[2,2,4,128]{3,2,1,0:T(4,128)S(1)} %copy-done, bf16[320,144]{1,0:T(8,128)(2,1)S(1)} %concatenate.3.wall_ref, bf16[16,81]{1,0:T(8,128)(2,1)S(1)} %copy.33.w1_ref, bf16[16,162]{1,0:T(8,128)(2,1)S(1)} %copy.34.w3t_ref, ...), custom_call_target="tpu_custom_call" | custom-call | tf_op jit(solution)/shard_map/pallas_call | solution.py:323
  38.0 120.2 %all-reduce.2.cloned.1.call-done = f32[184,144]{1,0:T(8,128)} async-done(((f32[184,144]{1,0:T(8,128)}), f32[184,144]{1,0:T(8,128)}) %all-reduce.2.cloned.1.call-update) | async-done | bytes 106000 | tf_op jit(solution)/shard_map/psum | solution.py:352
  158.2 0.9 broadcast_multiply_fusion
  159.2 0.6 slice.38
  159.8 0.7 slice_reduce_fusion.2
  160.5 0.7 slice_reduce_fusion
  161.3 0.7 copy.39
  162.0 0.1 reshape.56
  162.1 0.7 copy.42
  162.8 0.2 slice-done
  163.0 0.4 reshape.55
  163.4 0.9 copy.40
  164.3 0.6 copy.46
  164.9 0.6 copy.47
  (35 shorter events, 1.0 us)
Async XLA Ops:
  7.2 0.7 copy-start.6
  7.2 151.1 %all-reduce.2.cloned.1.call-start = ((), (), s32[]{:S(2)}) async-start(), calls=%async_computation | async-start | bytes 376832 | tf_op jit(solution)/shard_map/psum | solution.py:352
  7.9 0.7 copy-start.7
  8.7 0.9 copy-start.5
  9.5 0.8 copy-start.4
  9.6 1.1 copy-start.2
  11.6 0.7 copy-start
  11.6 0.7 copy-start.1
  159.2 2.0 %copy-start.3 = (f32[184,144]{1,0:T(8,128)}, f32[184,144]{1,0:T(8,128)S(1)}, u32[]{:S(2)}) copy-start(f32[184,144]{1,0:T(8,128)S(1)} %broadcast_multiply_fusion) | copy-start | bytes 317956
  162.1 0.9 slice-start
Sparse Core Ops, SparseCore 0:
  38.2 120.0 all-reduce.1

commit v2 on v1

--- a/solution.py
+++ b/solution.py
@@ -13,6 +13,7 @@
 F32 = jnp.float32
 BF16 = jnp.bfloat16
 OFFSETS = [(dx, dy) for dx in range(-2, 3) for dy in range(-2, 3) if (dx, dy) != (0, 0)]
+CHUNKS = 26
 PAIRS = [(y, t) for y in range(2) for t in range(4)]
 
 
@@ -52,10 +53,11 @@
 
 def taps_single(y, t):
     lane = iota((1, 144), 1)
+    d = (lane >= 48).astype(jnp.int32) + (lane >= 96).astype(jnp.int32)
     b = ((lane >> 2) & 3) - y
     c = ((lane & 3) - t + 1) & 3
     ok = (b >= 0) & (b <= 2) & (c <= 2)
-    return select_matrix(81, jnp.where(ok, (lane >> 4) * 9 + b * 3 + c, -1))
+    return select_matrix(81, jnp.where(ok, ((lane >> 4) - 3 * d) * 27 + b * 9 + c * 3 + d, -1))
 
 
 def taps_heads(y, t):
@@ -75,12 +77,31 @@
 
 
 def kernel(
-    nx, ny, noise_ref, wall_ref, w1_ref, w3t_ref, b1_ref, b2_ref, b3_ref,
+    nx, ny, sites, noise_ref, wall_ref, w1_ref, w3t_ref, b1_ref, b2_ref, b3_ref,
     field_ref, ngrad_ref, pack_ref,
-    win, inr, clw, clr, g2, g2t, g1, g3t, h1, h2, cm, cf, fld,
-    send_a, recv_a, send_b, recv_b,
+    win, inr, clw, clr, g2, g2t, g1, g3t, h1, h2, cm, cf, fld, partial_ref, parts, total,
+    send_a, recv_a, send_b, recv_b, send_c, recv_c, send_d, recv_d,
 ):
     ix, iy = lax.axis_index("gx"), lax.axis_index("gy")
+    devices = nx * ny
+    me = ix * ny + iy
+
+    def place(index):
+        return (lax.div(index, ny), lax.rem(index, ny))
+
+    def contribute(chunks):
+        for c in chunks:
+            @pl.when(me != c)
+            def _():
+                slot = lax.rem(me - c - 1 + devices, devices)
+                pltpu.make_async_remote_copy(
+                    src_ref=partial_ref.at[pl.ds(8 * c, 8)],
+                    dst_ref=parts.at[pl.ds(pl.multiple_of(slot * 8, 8), 8)],
+                    send_sem=send_c.at[c],
+                    recv_sem=recv_c,
+                    device_id=(c // ny, c % ny),
+                    device_id_type=MESH,
+                ).start()
 
     def peer(dx, dy):
         return (lax.rem(ix + dx + 2 * nx, nx), lax.rem(iy + dy + 2 * ny, ny))
@@ -105,9 +126,15 @@
             win[pl.ds(16 + 4 * y, 4), pl.ds(512 + 128 * x, 128)] = noise_ref[x, y]
 
     barrier = pltpu.get_barrier_semaphore()
-    for dx, dy in OFFSETS:
-        pl.semaphore_signal(barrier, inc=1, device_id=peer(dx, dy), device_id_type=MESH)
-    pl.semaphore_wait(barrier, len(OFFSETS))
+
+    def greet(k, _):
+        pl.semaphore_signal(
+            barrier, inc=1, device_id=place(lax.rem(me + k, devices)), device_id_type=MESH
+        )
+        return 0
+
+    lax.fori_loop(1, devices, greet, 0)
+    pl.semaphore_wait(barrier, devices - 1)
     first = exchange(win, 8, send_a, recv_a)
     for copy in first:
         copy.start()
@@ -273,7 +300,11 @@
         matrix = taps_channels(y, t)
         part = dot_nt(high, matrix) + dot_nt(low, matrix)
         folded = part if folded is None else folded + part
-    pack_ref[pl.ds(0, 168), :] = folded
+    partial_ref[pl.ds(0, 168), :] = folded[:, :128]
+    partial_ref[pl.ds(184, 24), :] = jnp.concatenate(
+        [folded[24 * q : 24 * q + 24, 128:] for q in range(7)] + [jnp.zeros((24, 16), F32)], axis=1
+    )
+    contribute([c for c in range(CHUNKS) if c not in (21, 22)])
 
     for k in range(2):
         hidden = h1[pl.ds(128 * (k + 1), 128), pl.ds(256, 512)].astype(F32)
@@ -294,19 +325,89 @@
         part = dot_nt(high, matrix) + dot_nt(low, matrix)
         folded = part if folded is None else folded + part
     pad = jnp.zeros((14, 1), F32)
-    pack_ref[pl.ds(168, 16), :] = jnp.concatenate(
+    partial_ref[pl.ds(168, 16), :] = jnp.concatenate(
         [
             folded, bias_mid, bias_first, jnp.concatenate([bias_last, pad], axis=0),
-            jnp.concatenate([loss, pad, jnp.zeros((1, 1), F32)], axis=0), jnp.zeros((16, 59), F32),
+            jnp.concatenate([loss, pad, jnp.zeros((1, 1), F32)], axis=0), jnp.zeros((16, 43), F32),
         ],
         axis=1,
     )
+    contribute([21, 22])
 
     back = conv(g1t, cf, 0, 256, 8)
     result = jnp.where(frozen, back, 0.0) + force * jnp.where(frozen, 1.0, growth) - noise
     for x in range(2):
         for y in range(2):
             ngrad_ref[x, y] = result[4 * y : 4 * y + 4, 128 * x : 128 * x + 128]
+
+    @pl.when(me < CHUNKS)
+    def _():
+        pltpu.make_async_copy(parts, parts, recv_c).wait()
+        rows = pl.ds(pl.multiple_of(me * 8, 8), 8)
+        summed = partial_ref[rows, :]
+        for k in range(devices - 1):
+            summed = summed + parts[pl.ds(8 * k, 8), :]
+        total[rows, :] = summed / sites
+
+        def share(k, _):
+            pltpu.make_async_remote_copy(
+                src_ref=total.at[rows],
+                dst_ref=total.at[rows],
+                send_sem=send_d,
+                recv_sem=recv_d.at[me],
+                device_id=place(lax.rem(me + k, devices)),
+                device_id_type=MESH,
+            ).start()
+            return 0
+
+        lax.fori_loop(1, devices, share, 0)
+
+    for c in range(CHUNKS):
+        @pl.when(me != c)
+        def _():
+            pltpu.make_async_copy(
+                partial_ref.at[pl.ds(8 * c, 8)], partial_ref.at[pl.ds(8 * c, 8)], send_c.at[c]
+            ).wait()
+            pltpu.make_async_copy(
+                total.at[pl.ds(8 * c, 8)], total.at[pl.ds(8 * c, 8)], recv_d.at[c]
+            ).wait()
+
+    pack_ref[...] = total[...]
+
+    @pl.when(me < CHUNKS)
+    def _():
+        pltpu.make_async_copy(parts, parts, send_d).wait()
+
+
+def unpack(
+    pack_ref, field_ref, ngrad_ref,
+    field_out, ngrad_out, loss_out, w1_out, b1_out, w2_out, b2_out, w3_out, b3_out,
+):
+    field_out[...] = field_ref[...]
+    ngrad_out[...] = ngrad_ref[...]
+    last_taps = pack_ref[pl.ds(184, 24), :]
+    last_taps = jnp.concatenate(
+        [last_taps[:, 16 * q : 16 * q + 16] for q in range(7)], axis=0
+    )
+
+    def taps(start, rows, g):
+        if g == 8:
+            return last_taps[start : start + rows]
+        return pack_ref[pl.ds(start, rows), :][:, 16 * g : 16 * g + 16]
+
+    for a in range(3):
+        for g in range(9):
+            heads = taps(144 + 8 * a, 8, g)
+            for d in range(3):
+                w2_out[a, g // 3, g % 3, d] = taps((3 * a + d) * 16, 16, g)
+                w3_out[a, g // 3, g % 3, d] = heads[2 * d : 2 * d + 2]
+    extra = jnp.transpose(pack_ref[pl.ds(168, 16), :], (1, 0))
+    for r in range(81):
+        w1_out[r // 27, (r // 9) % 3, (r // 3) % 3, r % 3] = extra[r : r + 1]
+    b2_out[...] = extra[81:82]
+    b1_out[...] = extra[82:83]
+    b3_out[...] = extra[83:84, :2]
+    loss_out[...] = extra[84:85, :1]
 
 
 def local(nx, ny, noise, w_first, b_first, w_middle, b_middle, w_last, b_last):
@@ -316,16 +417,17 @@
     wl = jnp.transpose(w_last, (2, 5, 0, 3, 4, 1)).reshape(18, 144)
     wft = jnp.transpose(w_first[:, 0, ::-1, ::-1, ::-1, ::-1], (1, 4, 2, 3, 0)).reshape(9, 144)
     wall = jnp.concatenate([wm, wmt, wl, wft, jnp.zeros((5, 144), BF16)], axis=0)
-    w1 = jnp.transpose(w_first[:, 0], (0, 4, 1, 2, 3)).reshape(16, 81)
+    w1 = w_first.reshape(16, 81)
     w3t = jnp.transpose(w_last[:, :, ::-1, ::-1, ::-1, ::-1], (1, 5, 2, 0, 3, 4)).reshape(16, 162)
     vmem = pl.BlockSpec(memory_space=pltpu.VMEM)
     smem = pl.BlockSpec(memory_space=pltpu.SMEM)
+    devices = nx * ny
     field, ngrad, pack = pl.pallas_call(
-        functools.partial(kernel, nx, ny),
+        functools.partial(kernel, nx, ny, sites),
         out_shape=(
             jax.ShapeDtypeStruct(noise.shape, F32),
             jax.ShapeDtypeStruct(noise.shape, F32),
-            jax.ShapeDtypeStruct((184, 144), F32),
+            jax.ShapeDtypeStruct((8 * CHUNKS, 128), F32),
         ),
         in_specs=[vmem] * 6 + [smem],
         out_specs=(vmem, vmem, vmem),
@@ -343,21 +445,38 @@
             pltpu.VMEM((384, 768), BF16),
             pltpu.VMEM((256, 512), BF16),
             pltpu.VMEM((16, 512), F32),
+            pltpu.VMEM((8 * CHUNKS, 128), F32),
+            pltpu.VMEM((8 * (devices - 1), 128), F32),
+            pltpu.VMEM((8 * CHUNKS, 128), F32),
         ]
-        + [pltpu.SemaphoreType.DMA((24,))] * 4,
+        + [pltpu.SemaphoreType.DMA((24,))] * 4
+        + [pltpu.SemaphoreType.DMA((CHUNKS,)), pltpu.SemaphoreType.DMA] * 1
+        + [pltpu.SemaphoreType.DMA, pltpu.SemaphoreType.DMA((CHUNKS,))],
         compiler_params=pltpu.CompilerParams(
             collective_id=0, has_side_effects=True, vmem_limit_bytes=32 * 1024 * 1024
         ),
     )(noise, wall, w1, w3t, b_first[:, None], b_middle[:, None], b_last)
-    pack = lax.psum(pack, ("gx", "gy")) / sites
-    middle = jnp.transpose(pack[:144].reshape(3, 3, 16, 3, 3, 16), (2, 5, 0, 3, 4, 1))
-    last = jnp.transpose(
-        pack[144:168].reshape(3, 8, 3, 3, 16)[:, :6].reshape(3, 3, 2, 3, 3, 16), (2, 5, 0, 3, 4, 1)
-    )
-    extra = pack[168:184]
-    first = jnp.transpose(extra[:, :81].reshape(16, 3, 3, 3, 3), (0, 2, 3, 4, 1))[:, None]
+    field, ngrad, loss, first, bias1, middle, bias2, last, bias3 = pl.pallas_call(
+        unpack,
+        out_shape=(
+            jax.ShapeDtypeStruct(noise.shape, F32),
+            jax.ShapeDtypeStruct(noise.shape, F32),
+            jax.ShapeDtypeStruct((1, 1), F32),
+            jax.ShapeDtypeStruct((3, 3, 3, 3, 1, 16), F32),
+            jax.ShapeDtypeStruct((1, 16), F32),
+            jax.ShapeDtypeStruct((3, 3, 3, 3, 16, 16), F32),
+            jax.ShapeDtypeStruct((1, 16), F32),
+            jax.ShapeDtypeStruct((3, 3, 3, 3, 2, 16), F32),
+            jax.ShapeDtypeStruct((1, 2), F32),
+        ),
+        in_specs=[vmem] * 3,
+        out_specs=(vmem,) * 9,
+    )(pack, field, ngrad)
+    order = (4, 5, 0, 1, 2, 3)
     return (
-        field, ngrad, extra[0, 84], first, extra[:, 82], middle, extra[:, 81], last, extra[:2, 83],
+        field, ngrad, loss.reshape(()), jnp.transpose(first, (5, 4, 0, 1, 2, 3)),
+        bias1.reshape(16), jnp.transpose(middle, order), bias2.reshape(16),
+        jnp.transpose(last, order), bias3.reshape(2),
     )
 
 

time: 173 us -> 45 us (0.26)
  waiting for transfers between devices: 120 us -> 0 us
  between operations: 14.2 us -> 0.77 us
  Pallas kernels: 25.7 us -> 37.3 us
  local copies, waits for them, and re-layouts: 11.3 us -> 6.6 us
    psum x1 -> x0, waiting for transfers between devices: 120 us -> none  [local(): pack = lax.psum(pack, ('gx', 'gy')) / sites]
    pallas_call x1 -> x2, Pallas kernels: 25.7 us -> 37.3 us  [the longest x1 35.3 us: local(): pl.pallas_call(functools.partial(kernel, nx, ny, sites), out_shape=(jax.S...]
    slice x9 -> x0, local copies, waits for them, and re-layouts: 2.32 us -> none  [the longest x1 0.7 us: local(): extra[:, 81]]
  transfers between devices with their start and end apart: 1 -> 0, of which waited for: 1 -> 0; matrix products, arithmetic and copies ran while one was open for 0% -> 0% of each run, Pallas kernels for 0% -> 0%
where the time goes in v2:
time: 45 us; the launch traced here: 44.7 us
  Pallas kernels  37.3 us (83%)
  local copies, waits for them, and re-layouts  6.6 us (15%)
  between operations  0.77 us (2%)
    pallas_call x1, Pallas kernels, local(): pl.pallas_call(functools.partial(kernel, nx, ny, sites), out_shape=(jax.S...  35.3 us
    unnamed x20, local copies, waits for them, and re-layouts  3.94 us
    pallas_call x1, Pallas kernels, local(): pl.pallas_call(unpack, out_shape=(jax.ShapeDtypeStruct(noise.shape, F32),...  2.02 us
    reshape x2, local copies, waits for them, and re-layouts, local(): w1 = w_first.reshape(16, 81)  0.92 us

profile of v2, /device:TPU:0, one launch (start us, length us, event | category | flops | bytes accessed | tf_op | source)
XLA Modules:
  0.0 44.7 jit_solution(6198108506798199018)
XLA Ops:
  0.7 0.6 %copy-done.8 = f32[16]{0:T(128)S(1)} copy-done((f32[16]{0:T(128)S(1)}, f32[16]{0:T(128)}, u32[]{:S(2)}) %copy-start.8) | copy-done | bytes 88
  1.3 0.1 copy.31.b1_ref
  1.4 0.6 %copy-done.9 = f32[16]{0:T(128)S(1)} copy-done((f32[16]{0:T(128)S(1)}, f32[16]{0:T(128)}, u32[]{:S(2)}) %copy-start.9) | copy-done | bytes 88
  2.0 0.1 copy.32.b2_ref
  2.0 0.8 %reshape.52 = bf16[16,81]{0,1:T(8,128)(2,1)S(1)} reshape(bf16[16,1,3,3,3,3]{0,5,4,3,2,1:T(4,128)(2,1)} %param.8) | data formatting | bytes 5184 | tf_op jit(solution)/shard_map/reshape | solution.py:420
  2.9 0.1 copy.29.w1_ref
  3.0 0.1 rev.10
  3.1 0.1 reshape.51
  3.3 0.1 copy.30.w3t_ref
  3.4 0.1 reshape.50
  3.5 0.4 copy-done.5
  3.9 0.2 copy.25
  4.1 0.2 reshape.49
  4.4 0.2 copy.24
  4.6 0.2 reshape.48
  4.8 0.0 copy-start.1
  4.8 0.0 copy-start.4
  4.9 0.2 concatenate.3.wall_ref
  5.0 0.5 %copy-done.1 = f32[2,2,4,128]{3,2,1,0:T(4,128)S(1)} copy-done((f32[2,2,4,128]{3,2,1,0:T(4,128)S(1)}, f32[2,2,4,128]{3,2,1,0:T(4,128)}, u32[]{:S(2)}) %copy-start.1) | copy-done | bytes 8216
  5.5 35.3 %shard_map.142 = (f32[2,2,4,128]{3,2,1,0:T(4,128)S(1)}, f32[2,2,4,128]{3,2,1,0:T(4,128)S(1)}, f32[208,128]{1,0:T(8,128)S(1)}) custom-call(f32[2,2,4,128]{3,2,1,0:T(4,128)S(1)} %copy-done.1, bf16[320,144]{1,0:T(8,128)(2,1)S(1)} %concatenate.3.wall_ref, bf16[16,81]{1,0:T(8,128)(2,1)S(1)} %copy.29.w1_ref, bf16[16,162]{1,0:T(8,128)(2,1)S(1)} %copy.30.w3t_ref, ...), custom_call_target="tpu_custom_call" | custom-call | tf_op jit(solution)/shard_map/pallas_call | solution.py:425
  40.8 0.6 %copy-done = f32[208,128]{1,0:T(8,128)} copy-done((f32[208,128]{1,0:T(8,128)}, f32[208,128]{1,0:T(8,128)S(1)}, u32[]{:S(2)}) %copy-start) | copy-done | bytes 106520
  41.5 0.6 %copy-done.2 = f32[2,2,4,128]{3,2,1,0:T(4,128)} copy-done((f32[2,2,4,128]{3,2,1,0:T(4,128)}, f32[2,2,4,128]{3,2,1,0:T(4,128)S(1)}, u32[]{:S(2)}) %copy-start.2) | copy-done | bytes 8216
  42.1 0.6 %copy-done.3 = f32[2,2,4,128]{3,2,1,0:T(4,128)} copy-done((f32[2,2,4,128]{3,2,1,0:T(4,128)}, f32[2,2,4,128]{3,2,1,0:T(4,128)S(1)}, u32[]{:S(2)}) %copy-start.3) | copy-done | bytes 8216
  42.6 2.0 %shard_map.143 = (f32[2,2,4,128]{3,2,1,0:T(4,128)}, f32[2,2,4,128]{3,2,1,0:T(4,128)}, f32[1,1]{1,0:T(1,128)}, f32[3,3,3,3,1,16]{5,4,3,2,1,0:T(1,128)}, f32[1,16]...) custom-call(f32[208,128]{1,0:T(8,128)} %copy-done, ...), custom_call_target="tpu_custom_call" | custom-call | tf_op jit(solution)/shard_map/pallas_call | solution.py:459
  (18 shorter events, 0.2 us)
Async XLA Ops:
  0.6 0.7 %copy-start.8 = (f32[16]{0:T(128)S(1)}, f32[16]{0:T(128)}, u32[]{:S(2)}) copy-start(f32[16]{0:T(128)} %param.9) | copy-start | bytes 196
  1.3 0.7 %copy-start.9 = (f32[16]{0:T(128)S(1)}, f32[16]{0:T(128)}, u32[]{:S(2)}) copy-start(f32[16]{0:T(128)} %param.11) | copy-start | bytes 196
  2.0 0.9 %copy-start.7 = (bf16[16,1,3,3,3,3]{0,5,4,3,2,1:T(4,128)(2,1)S(1)}, bf16[16,1,3,3,3,3]{0,5,4,3,2,1:T(4,128)(2,1)}, u32[]{:S(2)}) copy-start(bf16[16,1,3,3,3,3]{0,5,4,3,2,1:T(4,128)(2,1)} %param.8) | copy-start | bytes 7780
  2.0 1.1 %copy-start.6 = (bf16[2,16,3,3,3,3]{1,0,5,4,3,2:T(2,128)(2,1)S(1)}, bf16[2,16,3,3,3,3]{1,0,5,4,3,2:T(2,128)(2,1)}, u32[]{:S(2)}) copy-start(bf16[2,16,3,3,3,3]{1,0,5,4,3,2:T(2,128)(2,1)} %param.12) | copy-start | bytes 15556
  2.9 1.0 %copy-start.5 = (bf16[16,16,3,3,3,3]{1,0,5,4,3,2:T(8,128)(2,1)S(1)}, bf16[16,16,3,3,3,3]{1,0,5,4,3,2:T(8,128)(2,1)}, u32[]{:S(2)}) copy-start(bf16[16,16,3,3,3,3]{1,0,5,4,3,2:T(8,128)(2,1)} %param.10) | copy-start | bytes 124420
  4.8 0.7 %copy-start.1 = (f32[2,2,4,128]{3,2,1,0:T(4,128)S(1)}, f32[2,2,4,128]{3,2,1,0:T(4,128)}, u32[]{:S(2)}) copy-start(f32[2,2,4,128]{3,2,1,0:T(4,128)} %noise_ref.1) | copy-start | bytes 24580
  4.8 0.7 %copy-start.4 = (f32[2]{0:T(128)S(1)}, f32[2]{0:T(128)}, u32[]{:S(2)}) copy-start(f32[2]{0:T(128)} %b3_ref.1) | copy-start | bytes 28
  40.8 0.6 %copy-start = (f32[208,128]{1,0:T(8,128)}, f32[208,128]{1,0:T(8,128)S(1)}, u32[]{:S(2)}) copy-start(f32[208,128]{1,0:T(8,128)S(1)} %get-tuple-element.21.pack_ref) | copy-start | bytes 319492
  41.5 0.6 %copy-start.2 = (f32[2,2,4,128]{3,2,1,0:T(4,128)}, f32[2,2,4,128]{3,2,1,0:T(4,128)S(1)}, u32[]{:S(2)}) copy-start(f32[2,2,4,128]{3,2,1,0:T(4,128)S(1)} %get-tuple-element.22.field_ref) | copy-start | bytes 24580
  42.1 0.6 %copy-start.3 = (f32[2,2,4,128]{3,2,1,0:T(4,128)}, f32[2,2,4,128]{3,2,1,0:T(4,128)S(1)}, u32[]{:S(2)}) copy-start(f32[2,2,4,128]{3,2,1,0:T(4,128)S(1)} %get-tuple-element.23.ngrad_ref) | copy-start | bytes 24580

commit v3 on v2

--- a/solution.py
+++ b/solution.py
@@ -13,7 +13,7 @@
 F32 = jnp.float32
 BF16 = jnp.bfloat16
 OFFSETS = [(dx, dy) for dx in range(-2, 3) for dy in range(-2, 3) if (dx, dy) != (0, 0)]
-CHUNKS = 26
+CHUNKS = 12
 PAIRS = [(y, t) for y in range(2) for t in range(4)]
 
 
@@ -78,9 +78,10 @@
 
 def kernel(
     nx, ny, sites, noise_ref, wall_ref, w1_ref, w3t_ref, b1_ref, b2_ref, b3_ref,
-    field_ref, ngrad_ref, pack_ref,
-    win, inr, clw, clr, g2, g2t, g1, g3t, h1, h2, cm, cf, fld, partial_ref, parts, total,
-    send_a, recv_a, send_b, recv_b, send_c, recv_c, send_d, recv_d,
+    pack_ref,
+    win, inr, clw, clr, g2, g2t, g1, g3t, h1, h2, cm, cf, fld, tp,
+    partial_ref, parts, total, extra_ref, extra_parts, extra_total,
+    send_a, recv_a, send_b, recv_b, send_c, recv_c, recv_d, send_d, recv_e, send_f,
 ):
     ix, iy = lax.axis_index("gx"), lax.axis_index("gy")
     devices = nx * ny
@@ -89,19 +90,35 @@
     def place(index):
         return (lax.div(index, ny), lax.rem(index, ny))
 
-    def contribute(chunks):
-        for c in chunks:
-            @pl.when(me != c)
-            def _():
-                slot = lax.rem(me - c - 1 + devices, devices)
-                pltpu.make_async_remote_copy(
-                    src_ref=partial_ref.at[pl.ds(8 * c, 8)],
-                    dst_ref=parts.at[pl.ds(pl.multiple_of(slot * 8, 8), 8)],
-                    send_sem=send_c.at[c],
-                    recv_sem=recv_c,
-                    device_id=(c // ny, c % ny),
-                    device_id_type=MESH,
-                ).start()
+    def owner(c):
+        return c * devices // (CHUNKS + 1)
+
+    def contribute(c, source, buffer, arrived):
+        @pl.when(me != owner(c))
+        def _():
+            slot = lax.rem(me - owner(c) - 1 + devices, devices)
+            pltpu.make_async_remote_copy(
+                src_ref=source,
+                dst_ref=buffer.at[pl.ds(pl.multiple_of(slot * 16, 16), 16)],
+                send_sem=send_c.at[c],
+                recv_sem=arrived,
+                device_id=(owner(c) // ny, owner(c) % ny),
+                device_id_type=MESH,
+            ).start()
+
+    def share(c, ref, sent):
+        def step(k, _):
+            pltpu.make_async_remote_copy(
+                src_ref=ref,
+                dst_ref=ref,
+                send_sem=sent,
+                recv_sem=recv_d.at[c],
+                device_id=place(lax.rem(me + k, devices)),
+                device_id_type=MESH,
+            ).start()
+            return 0
+
+        lax.fori_loop(1, devices, step, 0)
 
     def peer(dx, dy):
         return (lax.rem(ix + dx + 2 * nx, nx), lax.rem(iy + dy + 2 * ny, ny))
@@ -109,6 +126,8 @@
     def exchange(ref, rows, send, recv):
         copies = []
         for k, (dx, dy) in enumerate(OFFSETS):
+            if dx == 2 and nx == 4:
+                continue
             copies.append(
                 pltpu.make_async_remote_copy(
                     src_ref=ref.at[pl.ds(2 * rows, rows), pl.ds(512, 256)],
@@ -144,11 +163,14 @@
     w3t = w3t_ref[...]
     small = []
     for n, (y, t) in enumerate(PAIRS):
-        full = dot(wall, taps_channels(y, t)).astype(BF16)
+        matrix = taps_channels(y, t)
+        tp[:, pl.ds(256 * n, 256)] = matrix
+        full = dot(wall, matrix).astype(BF16)
         for a in range(3):
             for d in range(3):
-                g2[a, pl.ds(d * 128 + n * 16, 16), :] = full[(3 * a + d) * 16 : (3 * a + d) * 16 + 16]
-                g2t[a, pl.ds(d * 128 + n * 16, 16), :] = full[
+                where = (pl.ds(d * 128 + n * 16, 16), pl.ds(256 * a, 256))
+                g2[where] = full[(3 * a + d) * 16 : (3 * a + d) * 16 + 16]
+                g2t[where] = full[
                     144 + (3 * a + d) * 16 : 144 + (3 * a + d) * 16 + 16
                 ]
         small.append(full[288:320])
@@ -158,14 +180,16 @@
     row = iota((216, 256), 0)
     order = jnp.where((row & 7) * 32 + (row >> 3) == iota((216, 256), 1), 1.0, 0.0).astype(BF16)
     small = dot(order, small).astype(BF16)
-    g3 = [small[48 * a : 48 * a + 48] for a in range(3)]
-    g1t = [small[144 + 24 * a : 168 + 24 * a] for a in range(3)]
+    g3 = jnp.concatenate([small[48 * a : 48 * a + 48] for a in range(3)], axis=1)
+    g1t = jnp.concatenate([small[144 + 24 * a : 168 + 24 * a] for a in range(3)], axis=1)
     b1, b2 = b1_ref[...], b2_ref[...]
     bias1 = jnp.concatenate([b1] * 8, axis=0)
     bias2 = jnp.concatenate([b2] * 8, axis=0)
 
     for copy in first:
         copy.wait()
+    if nx == 4:
+        win[:, pl.ds(0, 256)] = win[:, pl.ds(1024, 256)]
 
     noise_all = win[...]
     parity = (iota((40, 1280), 0) >> 2) + iota((40, 1280), 0) + (iota((40, 1280), 1) >> 7) + iota((40, 1280), 1)
@@ -184,10 +208,8 @@
         h1[pl.ds(128 * j, 128), :] = jnp.tanh(dot(g1[...], stack) + bias1).astype(BF16)
 
     def conv(mats, ref, start, width, rows):
-        out = None
-        for a in range(3):
-            part = dot(mats[a], ref[pl.ds(start, 256), pl.ds(128 * a, width)])
-            out = part if out is None else out + part
+        stack = [ref[pl.ds(start, 256), pl.ds(128 * a, width)] for a in range(3)]
+        out = dot(mats[...], jnp.concatenate(stack, axis=0))
         total = out[rows : 2 * rows]
         for d in (0, 2):
             total = total + roll_z(out[d * rows : (d + 1) * rows], d - 1)
@@ -246,7 +268,7 @@
         copy.start()
     for x in range(2):
         for y in range(2):
-            field_ref[x, y] = field[4 * y : 4 * y + 4, 128 * x : 128 * x + 128]
+            pack_ref[pl.ds(208 + 8 * x + 4 * y, 4), :] = field[4 * y : 4 * y + 4, 128 * x : 128 * x + 128]
 
     cot_f = cot_last.astype(F32)
     bias_last = jnp.sum(cot_f, axis=1, keepdims=True)
@@ -264,6 +286,8 @@
 
     for copy in second:
         copy.wait()
+    if nx == 4:
+        clw[:, pl.ds(0, 256)] = clw[:, pl.ds(1024, 256)]
 
     everywhere = clw[...].astype(F32)
     for d in range(3):
@@ -285,26 +309,34 @@
     bias_mid = sum(bias_mid[16 * n : 16 * n + 16] for n in range(8))
     turned = jnp.concatenate([roll_z(mine, 1 - d) for d in range(3)], axis=0).astype(BF16)
     products = [dot_nt(turned, h1[pl.ds(128, 256), pl.ds(128 * (a + 2), 256)]) for a in range(3)]
-    folded = None
-    for n, (y, t) in enumerate(PAIRS):
-        piece = jnp.concatenate(
-            [
-                products[a][d * 128 + n * 16 : d * 128 + n * 16 + 16]
-                for a in range(3)
-                for d in range(3)
-            ]
-            + [last_products[a][8 * n : 8 * n + 8] for a in range(3)],
-            axis=0,
+    pieces = []
+    for n in range(8):
+        pieces.append(
+            jnp.concatenate(
+                [
+                    products[a][d * 128 + n * 16 : d * 128 + n * 16 + 16]
+                    for a in range(3)
+                    for d in range(3)
+                ]
+                + [last_products[a][8 * n : 8 * n + 8] for a in range(3)],
+                axis=0,
+            )
         )
-        high, low = split(piece)
-        matrix = taps_channels(y, t)
-        part = dot_nt(high, matrix) + dot_nt(low, matrix)
-        folded = part if folded is None else folded + part
-    partial_ref[pl.ds(0, 168), :] = folded[:, :128]
-    partial_ref[pl.ds(184, 24), :] = jnp.concatenate(
-        [folded[24 * q : 24 * q + 24, 128:] for q in range(7)] + [jnp.zeros((24, 16), F32)], axis=1
-    )
-    contribute([c for c in range(CHUNKS) if c not in (21, 22)])
+    high, low = split(jnp.concatenate(pieces, axis=1))
+    folded = dot_nt(high, tp[...]) + dot_nt(low, tp[...])
+    partial_ref[pl.ds(0, 144), :] = folded[:144, :128].astype(BF16)
+    partial_ref[pl.ds(144, 48), :] = jnp.concatenate(
+        [
+            folded[144:, :128],
+            jnp.concatenate(
+                [folded[24 * q : 24 * q + 24, 128:] for q in range(7)] + [jnp.zeros((24, 16), F32)],
+                axis=1,
+            ),
+        ],
+        axis=0,
+    ).astype(BF16)
+    for c in range(CHUNKS):
+        contribute(c, partial_ref.at[pl.ds(16 * c, 16)], parts, recv_c)
 
     for k in range(2):
         hidden = h1[pl.ds(128 * (k + 1), 128), pl.ds(256, 512)].astype(F32)
@@ -325,67 +357,73 @@
         part = dot_nt(high, matrix) + dot_nt(low, matrix)
         folded = part if folded is None else folded + part
     pad = jnp.zeros((14, 1), F32)
-    partial_ref[pl.ds(168, 16), :] = jnp.concatenate(
+    extra_ref[...] = jnp.concatenate(
         [
             folded, bias_mid, bias_first, jnp.concatenate([bias_last, pad], axis=0),
             jnp.concatenate([loss, pad, jnp.zeros((1, 1), F32)], axis=0), jnp.zeros((16, 43), F32),
         ],
         axis=1,
     )
-    contribute([21, 22])
+    contribute(CHUNKS, extra_ref, extra_parts, recv_e)
 
     back = conv(g1t, cf, 0, 256, 8)
     result = jnp.where(frozen, back, 0.0) + force * jnp.where(frozen, 1.0, growth) - noise
     for x in range(2):
         for y in range(2):
-            ngrad_ref[x, y] = result[4 * y : 4 * y + 4, 128 * x : 128 * x + 128]
-
-    @pl.when(me < CHUNKS)
+            pack_ref[pl.ds(224 + 8 * x + 4 * y, 4), :] = result[4 * y : 4 * y + 4, 128 * x : 128 * x + 128]
+
+    def add_up(own, buffer, result):
+        summed = own.astype(F32)
+        for k in range(devices - 1):
+            summed = summed + buffer[pl.ds(16 * k, 16), :].astype(F32)
+        return (summed / sites).astype(result)
+
+    chunk = lax.div(me * (CHUNKS + 1) + devices - 1, devices)
+    owns = (lax.div(chunk * devices, CHUNKS + 1) == me) & (chunk < CHUNKS)
+    owns_extra = me == owner(CHUNKS)
+
+    @pl.when(owns)
     def _():
         pltpu.make_async_copy(parts, parts, recv_c).wait()
-        rows = pl.ds(pl.multiple_of(me * 8, 8), 8)
-        summed = partial_ref[rows, :]
-        for k in range(devices - 1):
-            summed = summed + parts[pl.ds(8 * k, 8), :]
-        total[rows, :] = summed / sites
-
-        def share(k, _):
-            pltpu.make_async_remote_copy(
-                src_ref=total.at[rows],
-                dst_ref=total.at[rows],
-                send_sem=send_d,
-                recv_sem=recv_d.at[me],
-                device_id=place(lax.rem(me + k, devices)),
-                device_id_type=MESH,
-            ).start()
-            return 0
-
-        lax.fori_loop(1, devices, share, 0)
-
-    for c in range(CHUNKS):
-        @pl.when(me != c)
+        rows = pl.ds(pl.multiple_of(chunk * 16, 16), 16)
+        total[rows, :] = add_up(partial_ref[rows, :], parts, BF16)
+        share(chunk, total.at[rows], send_d)
+
+    @pl.when(owns_extra)
+    def _():
+        pltpu.make_async_copy(extra_parts, extra_parts, recv_e).wait()
+        extra_total[...] = add_up(extra_ref[...], extra_parts, F32)
+        share(CHUNKS, extra_total, send_f)
+
+    for c in range(CHUNKS + 1):
+        @pl.when(me != owner(c))
         def _():
-            pltpu.make_async_copy(
-                partial_ref.at[pl.ds(8 * c, 8)], partial_ref.at[pl.ds(8 * c, 8)], send_c.at[c]
-            ).wait()
-            pltpu.make_async_copy(
-                total.at[pl.ds(8 * c, 8)], total.at[pl.ds(8 * c, 8)], recv_d.at[c]
-            ).wait()
-
-    pack_ref[...] = total[...]
-
-    @pl.when(me < CHUNKS)
+            sent = extra_ref if c == CHUNKS else partial_ref.at[pl.ds(16 * c, 16)]
+            given = extra_total if c == CHUNKS else total.at[pl.ds(16 * c, 16)]
+            pltpu.make_async_copy(sent, sent, send_c.at[c]).wait()
+            pltpu.make_async_copy(given, given, recv_d.at[c]).wait()
+
+    pack_ref[pl.ds(0, 192), :] = total[...].astype(F32)
+    pack_ref[pl.ds(192, 16), :] = extra_total[...]
+
+    @pl.when(owns)
     def _():
         pltpu.make_async_copy(parts, parts, send_d).wait()
 
+    @pl.when(owns_extra)
+    def _():
+        pltpu.make_async_copy(extra_parts, extra_parts, send_f).wait()
+
 
 def unpack(
-    pack_ref, field_ref, ngrad_ref,
+    pack_ref,
     field_out, ngrad_out, loss_out, w1_out, b1_out, w2_out, b2_out, w3_out, b3_out,
 ):
-    field_out[...] = field_ref[...]
-    ngrad_out[...] = ngrad_ref[...]
-    last_taps = pack_ref[pl.ds(184, 24), :]
+    for x in range(2):
+        for y in range(2):
+            field_out[x, y] = pack_ref[pl.ds(208 + 8 * x + 4 * y, 4), :]
+            ngrad_out[x, y] = pack_ref[pl.ds(224 + 8 * x + 4 * y, 4), :]
+    last_taps = pack_ref[pl.ds(168, 24), :]
     last_taps = jnp.concatenate(
         [last_taps[:, 16 * q : 16 * q + 16] for q in range(7)], axis=0
     )
@@ -401,7 +439,7 @@
             for d in range(3):
                 w2_out[a, g // 3, g % 3, d] = taps((3 * a + d) * 16, 16, g)
                 w3_out[a, g // 3, g % 3, d] = heads[2 * d : 2 * d + 2]
-    extra = jnp.transpose(pack_ref[pl.ds(168, 16), :], (1, 0))
+    extra = jnp.transpose(pack_ref[pl.ds(192, 16), :], (1, 0))
     for r in range(81):
         w1_out[r // 27, (r // 9) % 3, (r // 3) % 3, r % 3] = extra[r : r + 1]
     b2_out[...] = extra[81:82]
@@ -422,22 +460,18 @@
     vmem = pl.BlockSpec(memory_space=pltpu.VMEM)
     smem = pl.BlockSpec(memory_space=pltpu.SMEM)
     devices = nx * ny
-    field, ngrad, pack = pl.pallas_call(
+    pack = pl.pallas_call(
         functools.partial(kernel, nx, ny, sites),
-        out_shape=(
-            jax.ShapeDtypeStruct(noise.shape, F32),
-            jax.ShapeDtypeStruct(noise.shape, F32),
-            jax.ShapeDtypeStruct((8 * CHUNKS, 128), F32),
-        ),
+        out_shape=jax.ShapeDtypeStruct((240, 128), F32),
         in_specs=[vmem] * 6 + [smem],
-        out_specs=(vmem, vmem, vmem),
+        out_specs=vmem,
         scratch_shapes=[
             pltpu.VMEM((40, 1280), F32),
             pltpu.VMEM((3, 40, 1280), F32),
             pltpu.VMEM((80, 1280), BF16),
             pltpu.VMEM((3, 80, 1280), BF16),
-            pltpu.VMEM((3, 384, 256), BF16),
-            pltpu.VMEM((3, 384, 256), BF16),
+            pltpu.VMEM((384, 768), BF16),
+            pltpu.VMEM((384, 768), BF16),
             pltpu.VMEM((128, 144), BF16),
             pltpu.VMEM((128, 432), BF16),
             pltpu.VMEM((512, 1024), BF16),
@@ -445,13 +479,17 @@
             pltpu.VMEM((384, 768), BF16),
             pltpu.VMEM((256, 512), BF16),
             pltpu.VMEM((16, 512), F32),
-            pltpu.VMEM((8 * CHUNKS, 128), F32),
-            pltpu.VMEM((8 * (devices - 1), 128), F32),
-            pltpu.VMEM((8 * CHUNKS, 128), F32),
+            pltpu.VMEM((144, 2048), BF16),
+            pltpu.VMEM((16 * CHUNKS, 128), BF16),
+            pltpu.VMEM((16 * (devices - 1), 128), BF16),
+            pltpu.VMEM((16 * CHUNKS, 128), BF16),
+            pltpu.VMEM((16, 128), F32),
+            pltpu.VMEM((16 * (devices - 1), 128), F32),
+            pltpu.VMEM((16, 128), F32),
         ]
         + [pltpu.SemaphoreType.DMA((24,))] * 4
-        + [pltpu.SemaphoreType.DMA((CHUNKS,)), pltpu.SemaphoreType.DMA] * 1
-        + [pltpu.SemaphoreType.DMA, pltpu.SemaphoreType.DMA((CHUNKS,))],
+        + [pltpu.SemaphoreType.DMA((CHUNKS + 1,)), pltpu.SemaphoreType.DMA] * 2
+        + [pltpu.SemaphoreType.DMA] * 2,
         compiler_params=pltpu.CompilerParams(
             collective_id=0, has_side_effects=True, vmem_limit_bytes=32 * 1024 * 1024
         ),
@@ -469,9 +507,9 @@
             jax.ShapeDtypeStruct((3, 3, 3, 3, 2, 16), F32),
             jax.ShapeDtypeStruct((1, 2), F32),
         ),
-        in_specs=[vmem] * 3,
+        in_specs=[vmem],
         out_specs=(vmem,) * 9,
-    )(pack, field, ngrad)
+    )(pack)
     order = (4, 5, 0, 1, 2, 3)
     return (
         field, ngrad, loss.reshape(()), jnp.transpose(first, (5, 4, 0, 1, 2, 3)),

time: 45 us -> 41.5 us (0.922)
  Pallas kernels: 37.3 us -> 35.1 us
  local copies, waits for them, and re-layouts: 6.6 us -> 5.43 us
    pallas_call x1, Pallas kernels: 35.3 us -> 33 us  [local(): pl.pallas_call(functools.partial(kernel, nx, ny, sites), out_shape=jax.Sh...]
    unnamed x20 -> x16, local copies, waits for them, and re-layouts: 3.94 us -> 2.77 us
where the time goes in v3:
time: 41.5 us; the launch traced here: 41.3 us
  Pallas kernels  35.1 us (85%)
  local copies, waits for them, and re-layouts  5.43 us (13%)
  between operations  0.76 us (2%)
    pallas_call x1, Pallas kernels, local(): pl.pallas_call(functools.partial(kernel, nx, ny, sites), out_shape=jax.Sh...  33 us
    unnamed x16, local copies, waits for them, and re-layouts  2.77 us
    pallas_call x1, Pallas kernels, local(): pl.pallas_call(unpack, out_shape=(jax.ShapeDtypeStruct(noise.shape, F32),...  2.01 us
    reshape x2, local copies, waits for them, and re-layouts, local(): w1 = w_first.reshape(16, 81)  0.92 us

profile of v3, /device:TPU:0, one launch (start us, length us, event | category | flops | bytes accessed | tf_op | source)
XLA Modules:
  0.0 41.3 jit_solution(12686872993804296393)
XLA Ops:
  0.7 0.6 %copy-done.6 = f32[16]{0:T(128)S(1)} copy-done((f32[16]{0:T(128)S(1)}, f32[16]{0:T(128)}, u32[]{:S(2)}) %copy-start.6) | copy-done | bytes 88
  1.3 0.1 copy.31.b1_ref
  1.4 0.6 %copy-done.7 = f32[16]{0:T(128)S(1)} copy-done((f32[16]{0:T(128)S(1)}, f32[16]{0:T(128)}, u32[]{:S(2)}) %copy-start.7) | copy-done | bytes 88
  2.0 0.1 copy.32.b2_ref
  2.0 0.8 %reshape.52 = bf16[16,81]{0,1:T(8,128)(2,1)S(1)} reshape(bf16[16,1,3,3,3,3]{0,5,4,3,2,1:T(4,128)(2,1)} %param.8) | data formatting | bytes 5184 | tf_op jit(solution)/shard_map/reshape | solution.py:458
  2.9 0.0 copy-start.3
  2.9 0.1 copy.29.w1_ref
  3.0 0.1 rev.10
  3.1 0.1 reshape.51
  3.2 0.0 copy-done.4
  3.3 0.1 copy.30.w3t_ref
  3.4 0.1 reshape.50
  3.5 0.4 copy-done.3
  3.9 0.2 copy.25
  4.1 0.2 reshape.49
  4.4 0.2 copy.24
  4.6 0.2 reshape.48
  4.8 0.0 copy-start.1
  4.8 0.0 copy-start.2
  4.9 0.2 concatenate.3.wall_ref
  5.0 0.5 %copy-done.1 = f32[2,2,4,128]{3,2,1,0:T(4,128)S(1)} copy-done((f32[2,2,4,128]{3,2,1,0:T(4,128)S(1)}, f32[2,2,4,128]{3,2,1,0:T(4,128)}, u32[]{:S(2)}) %copy-start.1) | copy-done | bytes 8216
  5.5 33.0 %shard_map.142.pack_ref = f32[240,128]{1,0:T(8,128)S(1)} custom-call(f32[2,2,4,128]{3,2,1,0:T(4,128)S(1)} %copy-done.1, bf16[320,144]{1,0:T(8,128)(2,1)S(1)} %concatenate.3.wall_ref, bf16[16,81]{1,0:T(8,128)(2,1)S(1)} %copy.29.w1_ref, bf16[16,162]{1,0:T(8,128)(2,1)S(1)} %copy.30.w3t_ref, f32[16,1]{1,0:T(8,128)S(1)} %copy.31.b1_ref, ...), custom_call_target="tpu_custom_call" | custom-call | tf_op jit(solution)/shard_map/pallas_call | solution.py:463
  38.6 0.6 %copy-done = f32[240,128]{1,0:T(8,128)} copy-done((f32[240,128]{1,0:T(8,128)}, f32[240,128]{1,0:T(8,128)S(1)}, u32[]{:S(2)}) %copy-start) | copy-done | bytes 122904
  39.2 2.0 %shard_map.143 = (f32[2,2,4,128]{3,2,1,0:T(4,128)}, f32[2,2,4,128]{3,2,1,0:T(4,128)}, f32[1,1]{1,0:T(1,128)}, f32[3,3,3,3,1,16]{5,4,3,2,1,0:T(1,128)}, f32[1,16]...) custom-call(f32[240,128]{1,0:T(8,128)} %copy-done), custom_call_target="tpu_custom_call" | custom-call | tf_op jit(solution)/shard_map/pallas_call | solution.py:497
  (14 shorter events, 0.2 us)
Async XLA Ops:
  0.6 0.7 %copy-start.6 = (f32[16]{0:T(128)S(1)}, f32[16]{0:T(128)}, u32[]{:S(2)}) copy-start(f32[16]{0:T(128)} %param.9) | copy-start | bytes 196
  1.3 0.7 %copy-start.7 = (f32[16]{0:T(128)S(1)}, f32[16]{0:T(128)}, u32[]{:S(2)}) copy-start(f32[16]{0:T(128)} %param.11) | copy-start | bytes 196
  2.0 0.9 %copy-start.5 = (bf16[16,1,3,3,3,3]{0,5,4,3,2,1:T(4,128)(2,1)S(1)}, bf16[16,1,3,3,3,3]{0,5,4,3,2,1:T(4,128)(2,1)}, u32[]{:S(2)}) copy-start(bf16[16,1,3,3,3,3]{0,5,4,3,2,1:T(4,128)(2,1)} %param.8) | copy-start | bytes 7780
  2.0 1.1 %copy-start.4 = (bf16[2,16,3,3,3,3]{1,0,5,4,3,2:T(2,128)(2,1)S(1)}, bf16[2,16,3,3,3,3]{1,0,5,4,3,2:T(2,128)(2,1)}, u32[]{:S(2)}) copy-start(bf16[2,16,3,3,3,3]{1,0,5,4,3,2:T(2,128)(2,1)} %param.12) | copy-start | bytes 15556
  2.9 1.0 %copy-start.3 = (bf16[16,16,3,3,3,3]{1,0,5,4,3,2:T(8,128)(2,1)S(1)}, bf16[16,16,3,3,3,3]{1,0,5,4,3,2:T(8,128)(2,1)}, u32[]{:S(2)}) copy-start(bf16[16,16,3,3,3,3]{1,0,5,4,3,2:T(8,128)(2,1)} %param.10) | copy-start | bytes 124420
  4.8 0.7 %copy-start.1 = (f32[2,2,4,128]{3,2,1,0:T(4,128)S(1)}, f32[2,2,4,128]{3,2,1,0:T(4,128)}, u32[]{:S(2)}) copy-start(f32[2,2,4,128]{3,2,1,0:T(4,128)} %noise_ref.1) | copy-start | bytes 24580
  4.8 0.7 %copy-start.2 = (f32[2]{0:T(128)S(1)}, f32[2]{0:T(128)}, u32[]{:S(2)}) copy-start(f32[2]{0:T(128)} %b3_ref.1) | copy-start | bytes 28
  38.6 0.7 %copy-start = (f32[240,128]{1,0:T(8,128)}, f32[240,128]{1,0:T(8,128)S(1)}, u32[]{:S(2)}) copy-start(f32[240,128]{1,0:T(8,128)S(1)} %shard_map.142.pack_ref) | copy-start | bytes 368644

commit v4 on v3

--- a/solution.py
+++ b/solution.py
@@ -67,7 +67,7 @@
     b = 2 * (rest >> 4) + ((rest >> 2) & 1) - y - 1
     c = ((rest & 3) - t + 1) & 3
     ok = (b >= 0) & (b <= 2) & (c <= 2)
-    target = group * 18 + ((rest >> 3) & 1) * 9 + b * 3 + c
+    target = group * 18 + b * 6 + c * 2 + ((rest >> 3) & 1)
     return select_matrix(162, jnp.where(ok, target, -1))
 
 
@@ -77,11 +77,12 @@
 
 
 def kernel(
-    nx, ny, sites, noise_ref, wall_ref, w1_ref, w3t_ref, b1_ref, b2_ref, b3_ref,
+    nx, ny, sites, noise_hbm, w1_hbm, b1_hbm, w2_hbm, b2_hbm, w3_hbm, b3_hbm,
     pack_ref,
+    noise_ref, w1_ref, b1_ref, w2_ref, b2_ref, w3_ref, b3_ref, wall_ref, w1_rows, w3_rows,
     win, inr, clw, clr, g2, g2t, g1, g3t, h1, h2, cm, cf, fld, tp,
     partial_ref, parts, total, extra_ref, extra_parts, extra_total,
-    send_a, recv_a, send_b, recv_b, send_c, recv_c, recv_d, send_d, recv_e, send_f,
+    send_a, recv_a, send_b, recv_b, send_c, recv_c, recv_d, send_d, recv_e, send_f, load,
 ):
     ix, iy = lax.axis_index("gx"), lax.axis_index("gy")
     devices = nx * ny
@@ -140,10 +141,17 @@
             )
         return copies
 
-    for x in range(2):
-        for y in range(2):
-            win[pl.ds(16 + 4 * y, 4), pl.ds(512 + 128 * x, 128)] = noise_ref[x, y]
-
+    loads = [
+        pltpu.make_async_copy(source, target, load.at[k])
+        for k, (source, target) in enumerate(
+            [
+                (noise_hbm, noise_ref), (w1_hbm, w1_ref), (b1_hbm, b1_ref), (w2_hbm, w2_ref),
+                (b2_hbm, b2_ref), (w3_hbm, w3_ref), (b3_hbm, b3_ref),
+            ]
+        )
+    ]
+    for copy in loads:
+        copy.start()
     barrier = pltpu.get_barrier_semaphore()
 
     def greet(k, _):
@@ -153,14 +161,35 @@
         return 0
 
     lax.fori_loop(1, devices, greet, 0)
+    loads[0].wait()
+    for x in range(2):
+        for y in range(2):
+            win[pl.ds(16 + 4 * y, 4), pl.ds(512 + 128 * x, 128)] = noise_ref[x, y]
     pl.semaphore_wait(barrier, devices - 1)
     first = exchange(win, 8, send_a, recv_a)
     for copy in first:
         copy.start()
 
-    wall = wall_ref[...]
-    w1 = w1_ref[...]
-    w3t = w3t_ref[...]
+    for copy in loads[1:]:
+        copy.wait()
+    wall_ref[pl.ds(304, 16), :] = jnp.zeros((16, 144), F32)
+    for a in range(3):
+        for d in range(3):
+            slabs = [w2_ref[a, g // 3, g % 3, d].astype(F32) for g in range(9)]
+            wall_ref[pl.ds(16 * (3 * a + d), 16), :] = jnp.concatenate(slabs, axis=1)
+            turned = jnp.transpose(jnp.concatenate(slabs[::-1], axis=0), (1, 0))
+            wall_ref[pl.ds(144 + 16 * (3 * (2 - a) + 2 - d), 16), :] = turned
+            heads = [w3_ref[a, g // 3, g % 3, d].astype(F32) for g in range(9)]
+            wall_ref[pl.ds(288 + 2 * (3 * a + d), 2), :] = jnp.concatenate(heads, axis=1)
+            for g in range(9):
+                w3_rows[pl.ds((3 * (2 - d) + 2 - a) * 18 + 2 * (8 - g), 2), :] = heads[g]
+        for g in range(9):
+            row = w1_ref[0, a, g // 3, g % 3].astype(F32)
+            w1_rows[pl.ds(27 * a + 3 * g, 3), :] = row
+            wall_ref[pl.ds(306 + 3 * (2 - a), 3), pl.ds(16 * (8 - g), 16)] = row
+    wall = wall_ref[...].astype(BF16)
+    w1 = jnp.transpose(w1_rows[...], (1, 0))[:, :81].astype(BF16)
+    w3t = jnp.transpose(w3_rows[...], (1, 0))[:, :162].astype(BF16)
     small = []
     for n, (y, t) in enumerate(PAIRS):
         matrix = taps_channels(y, t)
@@ -179,10 +208,20 @@
     small = jnp.concatenate(small, axis=0)
     row = iota((216, 256), 0)
     order = jnp.where((row & 7) * 32 + (row >> 3) == iota((216, 256), 1), 1.0, 0.0).astype(BF16)
-    small = dot(order, small).astype(BF16)
-    g3 = jnp.concatenate([small[48 * a : 48 * a + 48] for a in range(3)], axis=1)
-    g1t = jnp.concatenate([small[144 + 24 * a : 168 + 24 * a] for a in range(3)], axis=1)
-    b1, b2 = b1_ref[...], b2_ref[...]
+    small = dot(order, small)
+    g3 = jnp.concatenate([small[48 * a : 48 * a + 48] for a in range(3)], axis=1).astype(BF16)
+    flipped = [
+        jnp.concatenate(
+            [small[144 + 24 * a + 8 * d : 152 + 24 * a + 8 * d] for d in (2, 1, 0)], axis=0
+        )
+        for a in range(3)
+    ]
+    g1t = jnp.concatenate(flipped, axis=1).astype(BF16)
+    eye = iota((16, 16), 0) == iota((16, 16), 1)
+    b1, b2 = (
+        jnp.sum(jnp.where(eye, jnp.broadcast_to(ref[...], (16, 16)), 0.0), axis=1, keepdims=True)
+        for ref in (b1_ref, b2_ref)
+    )
     bias1 = jnp.concatenate([b1] * 8, axis=0)
     bias2 = jnp.concatenate([b2] * 8, axis=0)
 
@@ -223,8 +262,8 @@
     scales, growths = [], []
     for k in range(2):
         head = conv(g3, h2, 128 * k, 512, 16)
-        log_scale = jnp.tanh(head[:8] + b3_ref[0])
-        offset = head[8:] + b3_ref[1]
+        log_scale = jnp.tanh(head[:8] + b3_ref[:, 0:1])
+        offset = head[8:] + b3_ref[:, 1:2]
         noise = win[pl.ds(12 + 8 * k, 8), pl.ds(384, 512)]
         growth = jnp.exp(log_scale)
         r, l = iota((8, 512), 0), iota((8, 512), 1)
@@ -450,22 +489,25 @@
 
 def local(nx, ny, noise, w_first, b_first, w_middle, b_middle, w_last, b_last):
     sites = float(noise.size * nx * ny)
-    wm = jnp.transpose(w_middle, (2, 5, 0, 3, 4, 1)).reshape(144, 144)
-    wmt = jnp.transpose(w_middle[:, :, ::-1, ::-1, ::-1, ::-1], (2, 5, 1, 3, 4, 0)).reshape(144, 144)
-    wl = jnp.transpose(w_last, (2, 5, 0, 3, 4, 1)).reshape(18, 144)
-    wft = jnp.transpose(w_first[:, 0, ::-1, ::-1, ::-1, ::-1], (1, 4, 2, 3, 0)).reshape(9, 144)
-    wall = jnp.concatenate([wm, wmt, wl, wft, jnp.zeros((5, 144), BF16)], axis=0)
-    w1 = w_first.reshape(16, 81)
-    w3t = jnp.transpose(w_last[:, :, ::-1, ::-1, ::-1, ::-1], (1, 5, 2, 0, 3, 4)).reshape(16, 162)
     vmem = pl.BlockSpec(memory_space=pltpu.VMEM)
-    smem = pl.BlockSpec(memory_space=pltpu.SMEM)
+    hbm = pl.BlockSpec(memory_space=pltpu.HBM)
     devices = nx * ny
     pack = pl.pallas_call(
         functools.partial(kernel, nx, ny, sites),
         out_shape=jax.ShapeDtypeStruct((240, 128), F32),
-        in_specs=[vmem] * 6 + [smem],
+        in_specs=[hbm] * 7,
         out_specs=vmem,
         scratch_shapes=[
+            pltpu.VMEM(noise.shape, F32),
+            pltpu.VMEM((1, 3, 3, 3, 3, 16), BF16),
+            pltpu.VMEM((1, 16), F32),
+            pltpu.VMEM((3, 3, 3, 3, 16, 16), BF16),
+            pltpu.VMEM((1, 16), F32),
+            pltpu.VMEM((3, 3, 3, 3, 2, 16), BF16),
+            pltpu.VMEM((1, 2), F32),
+            pltpu.VMEM((320, 144), F32),
+            pltpu.VMEM((128, 16), F32),
+            pltpu.VMEM((256, 16), F32),
             pltpu.VMEM((40, 1280), F32),
             pltpu.VMEM((3, 40, 1280), F32),
             pltpu.VMEM((80, 1280), BF16),
@@ -489,11 +531,16 @@
         ]
         + [pltpu.SemaphoreType.DMA((24,))] * 4
         + [pltpu.SemaphoreType.DMA((CHUNKS + 1,)), pltpu.SemaphoreType.DMA] * 2
-        + [pltpu.SemaphoreType.DMA] * 2,
+        + [pltpu.SemaphoreType.DMA] * 2
+        + [pltpu.SemaphoreType.DMA((7,))],
         compiler_params=pltpu.CompilerParams(
-            collective_id=0, has_side_effects=True, vmem_limit_bytes=32 * 1024 * 1024
+            collective_id=0, has_side_effects=True, vmem_limit_bytes=63 * 1024 * 1024
         ),
-    )(noise, wall, w1, w3t, b_first[:, None], b_middle[:, None], b_last)
+    )(
+        noise, jnp.transpose(w_first, (1, 2, 3, 4, 5, 0)), b_first.reshape(1, 16),
+        jnp.transpose(w_middle, (2, 3, 4, 5, 0, 1)), b_middle.reshape(1, 16),
+        jnp.transpose(w_last, (2, 3, 4, 5, 0, 1)), b_last.reshape(1, 2),
+    )
     field, ngrad, loss, first, bias1, middle, bias2, last, bias3 = pl.pallas_call(
         unpack,
         out_shape=(

time: 41.5 us -> 36.1 us (0.87)
  local copies, waits for them, and re-layouts: 5.43 us -> 0 us
    unnamed x16 -> x0, local copies, waits for them, and re-layouts: 2.77 us -> none
    reshape x8 -> x0, local copies, waits for them, and re-layouts: 1.72 us -> none  [the longest x2 0.92 us: local(): w1 = w_first.reshape(16, 81)]
    transpose x7 -> x0, local copies, waits for them, and re-layouts: 0.55 us -> none  [the longest x2 0.27 us: local(): jnp.transpose(w_middle[:, :, ::-1, ::-1, ::-1, ::-1], (2, 5, 1, 3, 4, 0))]
where the time goes in v4:
time: 36.1 us; the launch traced here: 35.9 us
  Pallas kernels  35.2 us (98%)
  between operations  0.65 us (2%)
    pallas_call x1, Pallas kernels, local(): pl.pallas_call(functools.partial(kernel, nx, ny, sites), out_shape=jax.Sh...  33.2 us
    pallas_call x1, Pallas kernels, local(): pl.pallas_call(unpack, out_shape=(jax.ShapeDtypeStruct(noise.shape, F32),...  2.01 us

profile of v4, /device:TPU:0, one launch (start us, length us, event | category | flops | bytes accessed | tf_op | source)
XLA Modules:
  0.0 35.9 jit_solution(3096196846962166986)
XLA Ops:
  0.6 33.2 %shard_map.142.pack_ref = f32[240,128]{1,0:T(8,128)} custom-call(f32[2,2,4,128]{3,2,1,0:T(4,128)} %noise_hbm.1, bf16[1,3,3,3,3,16]{5,4,3,2,1,0:T(4,128)(2,1)} %bitcast.15, f32[1,16]{1,0:T(1,128)} %bitcast.16, bf16[3,3,3,3,16,16]{5,4,3,2,1,0:T(8,128)(2,1)} %bitcast.13, f32[1,16]{1,0:T(1,128)} %bitcast.17, bf16[3,3,3,3,2,16]{5,4,3,2,1,0:T(2,128)(2,1)} %bitcast.14, ...), custom_call_target="tpu_custom_call" | custom-call | tf_op jit(solution)/shard_map/pallas_call | solution.py:495
  33.9 2.0 %shard_map.143 = (f32[2,2,4,128]{3,2,1,0:T(4,128)}, f32[2,2,4,128]{3,2,1,0:T(4,128)}, f32[1,1]{1,0:T(1,128)}, f32[3,3,3,3,1,16]{5,4,3,2,1,0:T(1,128)}, f32[1,16]...) custom-call(f32[240,128]{1,0:T(8,128)} %shard_map.142.pack_ref), custom_call_target="tpu_custom_call" | custom-call | tf_op jit(solution)/shard_map/pallas_call | solution.py:544

commit v5 on v4

--- a/solution.py
+++ b/solution.py
@@ -80,7 +80,7 @@
     nx, ny, sites, noise_hbm, w1_hbm, b1_hbm, w2_hbm, b2_hbm, w3_hbm, b3_hbm,
     pack_ref,
     noise_ref, w1_ref, b1_ref, w2_ref, b2_ref, w3_ref, b3_ref, wall_ref, w1_rows, w3_rows,
-    win, inr, clw, clr, g2, g2t, g1, g3t, h1, h2, cm, cf, fld, tp,
+    win, inr, clw, clr, g2, g2t, g1, g3t, h1, h2, cm, cf, fld, tp, ts,
     partial_ref, parts, total, extra_ref, extra_parts, extra_total,
     send_a, recv_a, send_b, recv_b, send_c, recv_c, recv_d, send_d, recv_e, send_f, load,
 ):
@@ -177,8 +177,6 @@
         for d in range(3):
             slabs = [w2_ref[a, g // 3, g % 3, d].astype(F32) for g in range(9)]
             wall_ref[pl.ds(16 * (3 * a + d), 16), :] = jnp.concatenate(slabs, axis=1)
-            turned = jnp.transpose(jnp.concatenate(slabs[::-1], axis=0), (1, 0))
-            wall_ref[pl.ds(144 + 16 * (3 * (2 - a) + 2 - d), 16), :] = turned
             heads = [w3_ref[a, g // 3, g % 3, d].astype(F32) for g in range(9)]
             wall_ref[pl.ds(288 + 2 * (3 * a + d), 2), :] = jnp.concatenate(heads, axis=1)
             for g in range(9):
@@ -187,9 +185,10 @@
             row = w1_ref[0, a, g // 3, g % 3].astype(F32)
             w1_rows[pl.ds(27 * a + 3 * g, 3), :] = row
             wall_ref[pl.ds(306 + 3 * (2 - a), 3), pl.ds(16 * (8 - g), 16)] = row
-    wall = wall_ref[...].astype(BF16)
+    wall = jnp.concatenate(
+        [wall_ref[pl.ds(0, 144), :], wall_ref[pl.ds(288, 32), :]], axis=0
+    ).astype(BF16)
     w1 = jnp.transpose(w1_rows[...], (1, 0))[:, :81].astype(BF16)
-    w3t = jnp.transpose(w3_rows[...], (1, 0))[:, :162].astype(BF16)
     small = []
     for n, (y, t) in enumerate(PAIRS):
         matrix = taps_channels(y, t)
@@ -199,12 +198,10 @@
             for d in range(3):
                 where = (pl.ds(d * 128 + n * 16, 16), pl.ds(256 * a, 256))
                 g2[where] = full[(3 * a + d) * 16 : (3 * a + d) * 16 + 16]
-                g2t[where] = full[
-                    144 + (3 * a + d) * 16 : 144 + (3 * a + d) * 16 + 16
-                ]
-        small.append(full[288:320])
-        g1[pl.ds(n * 16, 16), :] = dot(w1, taps_single(y, t)).astype(BF16)
-        g3t[pl.ds(n * 16, 16), :] = dot(w3t, taps_heads(y, t)).astype(BF16)
+        small.append(full[144:176])
+        single = taps_single(y, t)
+        ts[n] = single
+        g1[pl.ds(n * 16, 16), :] = dot(w1, single).astype(BF16)
     small = jnp.concatenate(small, axis=0)
     row = iota((216, 256), 0)
     order = jnp.where((row & 7) * 32 + (row >> 3) == iota((216, 256), 1), 1.0, 0.0).astype(BF16)
@@ -322,6 +319,22 @@
     last_products = [
         dot_nt(turned, h2[pl.ds(64, 256), pl.ds(128 * (a + 1), 256)]) for a in range(3)
     ]
+
+    for a in range(3):
+        for d in range(3):
+            slabs = [w2_ref[a, g // 3, g % 3, d].astype(F32) for g in range(8, -1, -1)]
+            wall_ref[pl.ds(144 + 16 * (3 * (2 - a) + 2 - d), 16), :] = jnp.transpose(
+                jnp.concatenate(slabs, axis=0), (1, 0)
+            )
+    wall = wall_ref[pl.ds(144, 144), :].astype(BF16)
+    w3t = jnp.transpose(w3_rows[...], (1, 0))[:, :162].astype(BF16)
+    for n, (y, t) in enumerate(PAIRS):
+        full = dot(wall, tp[:, pl.ds(256 * n, 256)]).astype(BF16)
+        for a in range(3):
+            for d in range(3):
+                where = (pl.ds(d * 128 + n * 16, 16), pl.ds(256 * a, 256))
+                g2t[where] = full[(3 * a + d) * 16 : (3 * a + d) * 16 + 16]
+        g3t[pl.ds(n * 16, 16), :] = dot(w3t, taps_heads(y, t)).astype(BF16)
 
     for copy in second:
         copy.wait()
@@ -392,7 +405,7 @@
     folded = None
     for n, (y, t) in enumerate(PAIRS):
         high, low = split(product[16 * n : 16 * n + 16])
-        matrix = taps_single(y, t)
+        matrix = ts[n]
         part = dot_nt(high, matrix) + dot_nt(low, matrix)
         folded = part if folded is None else folded + part
     pad = jnp.zeros((14, 1), F32)
@@ -405,12 +418,6 @@
     )
     contribute(CHUNKS, extra_ref, extra_parts, recv_e)
 
-    back = conv(g1t, cf, 0, 256, 8)
-    result = jnp.where(frozen, back, 0.0) + force * jnp.where(frozen, 1.0, growth) - noise
-    for x in range(2):
-        for y in range(2):
-            pack_ref[pl.ds(224 + 8 * x + 4 * y, 4), :] = result[4 * y : 4 * y + 4, 128 * x : 128 * x + 128]
-
     def add_up(own, buffer, result):
         summed = own.astype(F32)
         for k in range(devices - 1):
@@ -427,6 +434,12 @@
         rows = pl.ds(pl.multiple_of(chunk * 16, 16), 16)
         total[rows, :] = add_up(partial_ref[rows, :], parts, BF16)
         share(chunk, total.at[rows], send_d)
+
+    back = conv(g1t, cf, 0, 256, 8)
+    result = jnp.where(frozen, back, 0.0) + force * jnp.where(frozen, 1.0, growth) - noise
+    for x in range(2):
+        for y in range(2):
+            pack_ref[pl.ds(224 + 8 * x + 4 * y, 4), :] = result[4 * y : 4 * y + 4, 128 * x : 128 * x + 128]
 
     @pl.when(owns_extra)
     def _():
@@ -522,6 +535,7 @@
             pltpu.VMEM((256, 512), BF16),
             pltpu.VMEM((16, 512), F32),
             pltpu.VMEM((144, 2048), BF16),
+            pltpu.VMEM((8, 81, 144), BF16),
             pltpu.VMEM((16 * CHUNKS, 128), BF16),
             pltpu.VMEM((16 * (devices - 1), 128), BF16),
             pltpu.VMEM((16 * CHUNKS, 128), BF16),

time: 36.1 us -> 36.1 us (level)
  no operation moved by 1% of the time
where the time goes in v5:
time: 36.1 us; the launch traced here: 35.9 us
  Pallas kernels  35.2 us (98%)
  between operations  0.65 us (2%)
    pallas_call x1, Pallas kernels, local(): pl.pallas_call(functools.partial(kernel, nx, ny, sites), out_shape=jax.Sh...  33.2 us
    pallas_call x1, Pallas kernels, local(): pl.pallas_call(unpack, out_shape=(jax.ShapeDtypeStruct(noise.shape, F32),...  2.01 us

profile of v5, /device:TPU:0, one launch (start us, length us, event | category | flops | bytes accessed | tf_op | source)
XLA Modules:
  0.0 35.9 jit_solution(12925362168228594242)
XLA Ops:
  0.6 33.2 %shard_map.142.pack_ref = f32[240,128]{1,0:T(8,128)} custom-call(f32[2,2,4,128]{3,2,1,0:T(4,128)} %noise_hbm.1, bf16[1,3,3,3,3,16]{5,4,3,2,1,0:T(4,128)(2,1)} %bitcast.15, f32[1,16]{1,0:T(1,128)} %bitcast.16, bf16[3,3,3,3,16,16]{5,4,3,2,1,0:T(8,128)(2,1)} %bitcast.13, f32[1,16]{1,0:T(1,128)} %bitcast.17, bf16[3,3,3,3,2,16]{5,4,3,2,1,0:T(2,128)(2,1)} %bitcast.14, ...), custom_call_target="tpu_custom_call" | custom-call | tf_op jit(solution)/shard_map/pallas_call | solution.py:508
  33.9 2.0 %shard_map.143 = (f32[2,2,4,128]{3,2,1,0:T(4,128)}, f32[2,2,4,128]{3,2,1,0:T(4,128)}, f32[1,1]{1,0:T(1,128)}, f32[3,3,3,3,1,16]{5,4,3,2,1,0:T(1,128)}, f32[1,16]...) custom-call(f32[240,128]{1,0:T(8,128)} %shard_map.142.pack_ref), custom_call_target="tpu_custom_call" | custom-call | tf_op jit(solution)/shard_map/pallas_call | solution.py:558
